TPU v7x, 32 devices: a whole 2x2x4 slice. The times are simulated.
32 devices in a mesh: dp: 8 (over z, y), tensor: 4 (over x, core).
Axes of the slice: x: 2, y: 2, z: 4, core: 2. Of those that a mesh axis runs over, the one named last changes fastest.
Arguments:
- dense: bfloat16 [1536, 2048], P('dp'), may hold values from -8 to 8
- bottom_weight: bfloat16 [2048, 16384], P(None, 'tensor'), may hold values from -0.125 to 0.125
- bottom_bias: float32 [16384], P('tensor'), may hold values from -3 to 3
- cross_blocks: bfloat16 [40, 512, 512], P('tensor', 'dp'), may hold values from -0.25 to 0.25
- cross_bias: float32 [16384], P('tensor'), may hold values from -3 to 3
- cotangent: bfloat16 [1536, 16384], P('dp', 'tensor'), may hold values from -6 to 6
- in_blocks: int32 [4, 10], replicated, may hold values from 0 to 31, as said below
- out_blocks: int32 [4, 10], replicated, may hold values from 0 to 31, as said below
- live_slots: int32 [4], replicated, may hold values from 2 to 10, as said below
Outputs:
- cross_out: bfloat16 [1536, 16384], P('dp', 'tensor')
- grad_bottom: float32 [2048, 16384], P('dp', 'tensor')
- grad_bias_bottom: float32 [16384], P('tensor')
- grad_blocks: float32 [40, 512, 512], P('tensor', 'dp')
- grad_bias: float32 [16384], P('tensor')
Inputs may be any that keep to these rules, and one draw needn't show every extreme that they name: `in_blocks`: among the live slots of one tensor device, at most 3 have input blocks held by any one tensor device (blocks s * 16384 / (512 * 4) onward for device s), and this most is reached in every draw. `out_blocks`: among the live slots of one tensor device, at most 3 have output blocks held by any one tensor device, and this most is reached in every draw. `live_slots`: some tensor device has all 10 slots live.
All inputs are finite; a program needn't handle non-finite values.
Results may differ from a plain program's by a relative error of at most 0.014.
Values may be sent and summed in bfloat16 or wider, within the bound.
No kernel may reach another device: no remote copies, remote signals or barrier semaphores. Data moves between devices by JAX's collectives and lax.ppermute only.
A program may use at most 128 MiB of HBM per device.

v0:
```python
import jax
import jax.numpy as jnp
from jax import lax
from jax.sharding import PartitionSpec as P

BLK = 512
SLOTS = 10


def slot_ranks(owner, alive):
    order = jnp.arange(owner.shape[1])
    earlier = order[None, :] < order[:, None]
    same = (owner[:, :, None] == owner[:, None, :]) & alive[:, None, :] & earlier[None, :, :]
    return jnp.sum(same.astype(jnp.int32), axis=2)


def post_table(owner_mine, rank_mine, alive_mine, groups, capacity):
    slot_count = owner_mine.shape[0]
    match = (
        (owner_mine[None, None, :] == jnp.arange(groups)[:, None, None])
        & (rank_mine[None, None, :] == jnp.arange(capacity)[None, :, None])
        & alive_mine[None, None, :]
    )
    chosen = jnp.sum(match.astype(jnp.int32) * jnp.arange(slot_count)[None, None, :], axis=2)
    filled = jnp.any(match, axis=2)
    return (chosen, filled)


def pack_parts(parts, chosen, filled):
    picked = jnp.take(parts, chosen.reshape(-1), axis=1) * filled.reshape(-1)[None, :, None].astype(
        parts.dtype
    )
    return picked.reshape(parts.shape[0], chosen.shape[0], chosen.shape[1] * parts.shape[2])


def collect_parts(received, owner, local, rank, alive, target, capacity, per_device):
    row_count, groups, span_width = received.shape
    block_width = span_width // capacity
    match = ((owner == target) & alive)[:, :, None] & (
        rank[:, :, None] == jnp.arange(capacity)[None, None, :]
    )
    matches = match[:, :, :, None] & (
        local[:, :, None, None] == jnp.arange(per_device)[None, None, None, :]
    )
    onehot = (
        jnp.sum(matches.astype(jnp.int32), axis=1)
        .reshape(groups * capacity, per_device)
        .astype(jnp.bfloat16)
    )
    flattened = received.reshape(row_count, groups * capacity, block_width)
    summed = jnp.einsum("rib,il->rlb", flattened, onehot, preferred_element_type=jnp.float32)
    return summed.reshape(row_count, per_device * block_width)


def on_device(
    dense,
    bottom_weight,
    bottom_bias,
    cross_blocks,
    cross_bias,
    cotangent,
    in_blocks,
    out_blocks,
    live_slots,
):
    groups = lax.axis_size("tensor")
    mine = lax.axis_index("tensor")
    row_count = dense.shape[0]
    local_width = bottom_weight.shape[1]
    per_device = local_width // BLK
    capacity = -(-SLOTS // groups)
    preact = jnp.dot(dense, bottom_weight, preferred_element_type=jnp.float32) + bottom_bias
    start = jax.nn.silu(preact).astype(jnp.bfloat16)
    start_wide = start.astype(jnp.float32)
    cot_wide = cotangent.astype(jnp.float32)
    grad_mixed = cot_wide * start_wide
    grad_mixed_low = grad_mixed.astype(jnp.bfloat16)
    alive = jnp.arange(SLOTS)[None, :] < live_slots[:, None]
    alive_mine = alive[mine]
    switch = alive_mine.astype(jnp.bfloat16)[None, :, None]
    in_owner = in_blocks // per_device
    in_local = in_blocks % per_device
    out_owner = out_blocks // per_device
    out_local = out_blocks % per_device
    in_rank = slot_ranks(in_owner, alive)
    out_rank = slot_ranks(out_owner, alive)
    whole_start = lax.all_gather(start, "tensor", axis=1, tiled=True)
    fetched = jnp.take(whole_start.reshape(row_count, -1, BLK), in_blocks[mine], axis=1)
    taken = fetched
    product = jnp.einsum(
        "rki,kij->rkj",
        taken,
        lax.all_gather(cross_blocks, "dp", axis=1, tiled=True),
        preferred_element_type=jnp.float32,
    )
    parts = product.astype(jnp.bfloat16) * switch
    chosen_out, filled_out = post_table(
        out_owner[mine], out_rank[mine], alive_mine, groups, capacity
    )
    arrived_parts = lax.all_to_all(
        pack_parts(parts, chosen_out, filled_out), "tensor", split_axis=1, concat_axis=1, tiled=True
    )
    mixed = (
        collect_parts(
            arrived_parts, out_owner, out_local, out_rank, alive, mine, capacity, per_device
        )
        + cross_bias
    )
    cross_out = (start_wide * mixed + start_wide).astype(jnp.bfloat16)
    whole_grad = lax.all_gather(grad_mixed_low, "tensor", axis=1, tiled=True)
    upstream = jnp.take(whole_grad.reshape(row_count, -1, BLK), out_blocks[mine], axis=1)
    upstream = upstream * switch
    backward = jnp.einsum(
        "rkj,kij->rki",
        upstream,
        lax.all_gather(cross_blocks, "dp", axis=1, tiled=True),
        preferred_element_type=jnp.float32,
    )
    back_parts = backward.astype(jnp.bfloat16)
    chosen_in, filled_in = post_table(in_owner[mine], in_rank[mine], alive_mine, groups, capacity)
    arrived_back = lax.all_to_all(
        pack_parts(back_parts, chosen_in, filled_in),
        "tensor",
        split_axis=1,
        concat_axis=1,
        tiled=True,
    )
    grad_start = collect_parts(
        arrived_back, in_owner, in_local, in_rank, alive, mine, capacity, per_device
    )
    block_terms = jnp.einsum("rki,rkj->kij", fetched, upstream, preferred_element_type=jnp.float32)
    grad_blocks = lax.psum_scatter(
        block_terms.astype(jnp.bfloat16), "dp", scatter_dimension=1, tiled=True
    ).astype(jnp.float32)
    grad_start = grad_start + cot_wide * mixed + cot_wide
    sigma = jax.nn.sigmoid(preact)
    grad_pre = grad_start * sigma * (1.0 + preact * (1.0 - sigma))
    grad_pre_low = grad_pre.astype(jnp.bfloat16)
    taken = dense
    grad_bottom = lax.psum_scatter(
        lax.dot_general(
            taken, grad_pre_low, (((0,), (0,)), ((), ())), preferred_element_type=jnp.float32
        ).astype(jnp.bfloat16),
        "dp",
        scatter_dimension=0,
        tiled=True,
    ).astype(jnp.float32)
    bias_sums = lax.psum((jnp.sum(grad_pre, axis=0), jnp.sum(grad_mixed, axis=0)), "dp")
    return (cross_out, grad_bottom, bias_sums[0], grad_blocks, bias_sums[1])


def solution(mesh):
    return jax.shard_map(
        on_device,
        mesh=mesh,
        in_specs=(
            P("dp", None),
            P(None, "tensor"),
            P("tensor"),
            P("tensor", "dp", None),
            P("tensor"),
            P("dp", "tensor"),
            P(),
            P(),
            P(),
        ),
        out_specs=(
            P("dp", "tensor"),
            P("dp", "tensor"),
            P("tensor"),
            P("tensor", "dp", None),
            P("tensor"),
        ),
        check_vma=False,
    )
```

profile of v0, /device:TPU:0, one launch (start us, length us, event | category | flops | bytes accessed | tf_op | source)
XLA Modules:
  0.0 618.6 jit_solution(2519716006117630175)
XLA Ops:
  7.2 1.1 copy-done
  8.3 12.6 %fusion.4 = (f32[4096]{0:T(1024)S(1)}, bf16[192,4096]{1,0:T(8,128)(2,1)}, f32[192,4096]{1,0:T(8,128)}) fusion(bf16[192,4096]{1,0:T(8,128)(2,1)} %param.18, f32[4096]{0:T(1024)} %param.15, bf16[192,2048]{1,0:T(8,128)(2,1)S(1)} %copy-done, bf16[2048,4096]{1,0:T(8,128)(2,1)} %param.14), kind=kOutput, calls=%fused_computation.19 | convolution fusion | flops 3229085696 | bytes 23887872 | tf_op jit(solution)/shard_map/dot_general | solution.py:72
  21.0 1.3 copy-done.1
  22.3 3.1 fusion.5
  25.5 0.7 all-gather.6.cloned.1.call-update
  26.2 0.2 reduce-scatter.5.cloned.1.call-start
  26.6 43.6 %all-gather.4.cloned.1.call-done = bf16[192,16384]{1,0:T(8,128)(2,1)} async-done(((bf16[192,4096]{1,0:T(8,128)(2,1)}), bf16[192,16384]{1,0:T(8,128)(2,1)}) %all-gather.4.cloned.1.call-update) | async-done | bytes 6291472 | tf_op jit(solution)/shard_map/all_gather | solution.py:87
  70.2 6.3 %copy.84 = bf16[24,32,8,512]{3,2,0,1:T(8,128)(2,1)} copy(bf16[24,32,8,512]{3,2,1,0:T(8,128)(2,1)} %bitcast.72) | data formatting | bytes 12582912 | tf_op jit(solution)/shard_map/reshape | solution.py:88
  76.5 41.7 %all-gather.8.cloned.1.call-done = bf16[192,16384]{1,0:T(8,128)(2,1)} async-done(((bf16[192,4096]{1,0:T(8,128)(2,1)}), bf16[192,16384]{1,0:T(8,128)(2,1)}) %all-gather.8.cloned.1.call-update) | async-done | bytes 6291472 | tf_op jit(solution)/shard_map/all_gather | solution.py:110
  118.2 6.2 %copy.83 = bf16[24,32,8,512]{3,2,0,1:T(8,128)(2,1)} copy(bf16[24,32,8,512]{3,2,1,0:T(8,128)(2,1)} %bitcast.73) | data formatting | bytes 12582912 | tf_op jit(solution)/shard_map/reshape | solution.py:111
  124.4 4.8 gather_fusion
  129.2 5.0 gather_fusion.2
  134.2 6.5 %convolution_convert_fusion = bf16[10,512,512]{2,1,0:T(8,128)(2,1)} fusion(bf16[10,192,512]{2,1,0:T(8,128)(2,1)} %gather_fusion, pred[10]{0:T(512)(128)(4,1)S(1)} %get-tuple-element.65, bf16[10,192,512]{2,1,0:T(8,128)(2,1)} %gather_fusion.2, pred[10]{0:T(512)(128)(4,1)S(1)} %get-tuple-element.46, bf16[10]{0:T(256)(128)(2,1)S(1)} %get-tuple-element.52), kind=kOutput, calls=%fused_computation.18 | convolution fusion | flops 1012203520 | bytes 9175080 | tf_op jit(solution)/shard_map/rki,rkj->kij/dot_general | solution.py:131
  140.9 0.5 convert_reduce_fusion.2
  142.2 0.2 select_reduce_fusion
  142.8 63.9 %all-gather.6.cloned.1.call-done = bf16[10,512,512]{2,1,0:T(8,128)(2,1)} async-done(((bf16[10,64,512]{2,1,0:T(8,128)(2,1)}), bf16[10,512,512]{2,1,0:T(8,128)(2,1)}) %all-gather.6.cloned.1.call-update) | async-done | bytes 5242896 | tf_op jit(solution)/shard_map/all_gather | solution.py:93
  206.7 6.2 %convert_bitcast_fusion.1 = bf16[192,10,512]{2,0,1:T(8,128)(2,1)} fusion(bf16[10,512,512]{2,1,0:T(8,128)(2,1)} %all-gather.6.cloned.1.call-done, bf16[10,192,512]{2,1,0:T(8,128)(2,1)} %gather_fusion.2, pred[10]{0:T(512)(128)(4,1)S(1)} %get-tuple-element.46, bf16[10]{0:T(256)(128)(2,1)S(1)} %get-tuple-element.52), kind=kOutput, calls=%fused_computation.27 | convolution fusion | flops 1009582080 | bytes 9175070 | tf_op jit(solution)/shard_map/rkj,kij->rki/dot_general | solution.py:113
  212.9 3.7 gather_fusion.3
  216.6 1.9 bitcast_multiply_fusion
  218.6 3.1 copy.68
  221.7 6.2 %reshape.259 = bf16[192,4,1536]{2,1,0:T(4,128)(2,1)} reshape(bf16[192,12,512]{2,1,0:T(8,128)(2,1)} %copy.68) | data formatting | bytes 4718592 | tf_op jit(solution)/shard_map/reshape | solution.py:33
  227.9 3.5 copy.69
  231.4 4.7 all-to-all-start.1
  236.3 5.9 multiply_bitcast_fusion
  242.2 3.7 gather_fusion.1
  245.9 2.0 bitcast_multiply_fusion.1
  247.9 3.1 copy.59
  251.0 6.2 %reshape.254 = bf16[192,4,1536]{2,1,0:T(4,128)(2,1)} reshape(bf16[192,12,512]{2,1,0:T(8,128)(2,1)} %copy.59) | data formatting | bytes 4718592 | tf_op jit(solution)/shard_map/reshape | solution.py:33
  257.2 3.6 copy.60
  260.8 3.7 all-to-all-done.1
  264.5 4.5 all-to-all-start
  269.3 0.3 convert_reduce_fusion.1
  269.6 0.3 convert_reduce_fusion
  270.0 4.9 copy.70
  274.9 5.8 reshape.260
  280.7 2.5 fusion.14
  283.2 4.4 copy.80
  287.6 10.0 %all-to-all-done = bf16[192,4,1536]{2,0,1:T(8,128)(2,1)} async-done(((bf16[192,4,1536]{2,0,1:T(8,128)(2,1)}), bf16[192,4,1536]{2,0,1:T(8,128)(2,1)}, u32[]{:S(2)}, u32[]{:S(2)}) %all-to-all-start) | async-done | bytes 2359328 | tf_op jit(solution)/shard_map/all_to_all | solution.py:100
  297.6 5.0 copy.61
  302.6 5.8 reshape.255
  308.4 2.7 fusion.16
  311.1 2.8 copy.79
  313.9 3.2 fusion.28
  317.2 9.6 %convert_bitcast_fusion = bf16[2048,4096]{0,1:T(8,128)(2,1)} fusion(bf16[192,2048]{1,0:T(8,128)(2,1)S(1)} %copy-done, bf16[192,4096]{1,0:T(8,128)(2,1)} %get-tuple-element.43), kind=kOutput, calls=%fused_computation.4 | convolution fusion | flops 3229614080 | bytes 19136512 | tf_op jit(solution)/shard_map/dot_general | solution.py:141
  326.8 36.6 %all-reduce = (f32[4096]{0:T(1024)}, f32[4096]{0:T(1024)}) all-reduce(f32[4096]{0:T(1024)S(1)} %get-tuple-element.42, f32[4096]{0:T(1024)S(1)} %get-tuple-element.40), channel_id=1, replica_groups=mesh['dp'=8,'tensor'=4] {'dp'}, use_global_device_ids=true, to_apply=%region_10.13 | all-reduce | flops 8192 | bytes 65536 | tf_op jit(solution)/shard_map/psum | solution.py:148
  363.4 2.3 convert_element_type.136
  365.7 242.1 %reduce-scatter.3.cloned.1.call-done = bf16[256,4096]{0,1:T(8,128)(2,1)} async-done(((bf16[2048,4096]{0,1:T(8,128)(2,1)}), bf16[256,4096]{0,1:T(8,128)(2,1)}) %reduce-scatter.3.cloned.1.call-update) | async-done | bytes 2097168 | tf_op jit(solution)/shard_map/reduce_scatter | solution.py:140
  607.8 4.3 copy.72
  (66 shorter events, 2.2 us)
Async XLA Ops:
  7.2 1.1 copy-start
  7.2 63.0 %all-gather.4.cloned.1.call-start = ((), (), s32[]{:S(2)}) async-start(), calls=%async_computation.4 | async-start | bytes 7864320 | tf_op jit(solution)/shard_map/all_gather | solution.py:87
  20.9 1.4 copy-start.1
  21.0 5.5 copy-start.6
  21.0 5.5 copy-start.7
  21.0 5.5 copy-start.8
  21.0 97.2 %all-gather.8.cloned.1.call-start = ((), (), s32[]{:S(2)}) async-start(), calls=%async_computation.6 | async-start | bytes 7864320 | tf_op jit(solution)/shard_map/all_gather | solution.py:110
  25.5 181.2 %all-gather.6.cloned.1.call-start = ((), (), s32[]{:S(2)}) async-start(), calls=%async_computation.5 | async-start | bytes 5898240 | tf_op jit(solution)/shard_map/all_gather | solution.py:93
  26.2 337.2 %reduce-scatter.5.cloned.1.call-start = ((), (), s32[]{:S(2)}) async-start(), calls=%async_computation.8 | async-start | bytes 5898240 | tf_op jit(solution)/shard_map/reduce_scatter | solution.py:132
  231.4 33.1 %all-to-all-start.1 = ((bf16[192,4,1536]{2,0,1:T(8,128)(2,1)}), bf16[192,4,1536]{2,0,1:T(8,128)(2,1)}, u32[]{:S(2)}, u32[]{:S(2)}) async-start(bf16[192,4,1536]{2,0,1:T(8,128)(2,1)} %copy.69), calls=%async_computation.1 | async-start | bytes 4718592 | tf_op jit(solution)/shard_map/all_to_all | solution.py:121
  264.5 33.1 %all-to-all-start = ((bf16[192,4,1536]{2,0,1:T(8,128)(2,1)}), bf16[192,4,1536]{2,0,1:T(8,128)(2,1)}, u32[]{:S(2)}, u32[]{:S(2)}) async-start(bf16[192,4,1536]{2,0,1:T(8,128)(2,1)} %copy.60), calls=%async_computation | async-start | bytes 4718592 | tf_op jit(solution)/shard_map/all_to_all | solution.py:100
  269.0 338.8 %reduce-scatter.3.cloned.1.call-start = ((), (), s32[]{:S(2)}) async-start(), calls=%async_computation.7 | async-start | bytes 18874368 | tf_op jit(solution)/shard_map/reduce_scatter | solution.py:140
  308.4 5.5 copy-start.4
  311.1 2.8 copy-start.2
  311.1 2.8 copy-start.3
  311.1 2.8 copy-start.5
Sparse Core Ops, SparseCore 0:
  21.1 49.0 all-gather.3
  71.8 46.3 all-gather.7
  120.4 86.2 all-gather.5
  210.1 101.1 reduce-scatter.4
  326.9 280.8 reduce-scatter.2
where the time goes:
time: 620 us; the launch traced here: 619 us
  waiting for transfers between devices  406 us (65%)
  local copies, waits for them, and re-layouts  92.3 us (15%)
  matrix products  46 us (7%)
  blocking collectives  36.6 us (6%)
  other arithmetic  14.3 us (2%)
  between operations  14.1 us (2%)
  starting transfers between devices  9.65 us (2%)
    reduce_scatter x1, waiting for transfers between devices, on_device(): lax.psum_scatter(lax.dot_general(taken, grad_pre_low, (((0,), (0,)), ((),...  242 us
    all_gather x1, waiting for transfers between devices, on_device(): lax.all_gather(cross_blocks, 'dp', axis=1, tiled=True)  63.9 us
    all_gather x1, waiting for transfers between devices, on_device(): whole_start = lax.all_gather(start, 'tensor', axis=1, tiled=True)  43.6 us
    all_gather x1, waiting for transfers between devices, on_device(): whole_grad = lax.all_gather(grad_mixed_low, 'tensor', axis=1, tiled=True)  41.7 us
    psum x1, blocking collectives, on_device(): lax.psum((jnp.sum(grad_pre, axis=0), jnp.sum(grad_mixed, axis=0)), 'dp')  36.6 us
    reshape x4, local copies, waits for them, and re-layouts, pack_parts(): picked.reshape(parts.shape[0], chosen.shape[0], chosen.shape[1] * parts.s...  19.5 us
    unnamed x21, local copies, waits for them, and re-layouts  13.9 us
    dot_general x1, matrix products, on_device(): jnp.dot(dense, bottom_weight, preferred_element_type=jnp.float32)  12.6 us
  transfers between devices with their start and end apart: 7, of which 6 were waited for; matrix products, arithmetic and copies ran while one was open for 22% of the time, Pallas kernels for 0%

commit v1 on v0

v1 whole, which is shorter than its diff:
```python
import functools

import jax
import jax.numpy as jnp
import numpy as np
from jax import lax
from jax.experimental import pallas as pl
from jax.experimental.pallas import tpu as pltpu
from jax.sharding import Mesh, PartitionSpec as P

BLK = 512
SLOTS = 10
BF = jnp.bfloat16
F32 = jnp.float32
ANY = pl.BlockSpec(memory_space=pl.ANY)
VMEM = pl.BlockSpec(memory_space=pltpu.VMEM)
LIMIT = 56 * 1024 * 1024


def params(semantics=None):
    return pltpu.CompilerParams(vmem_limit_bytes=LIMIT, dimension_semantics=semantics)


def dot(a, b, dims):
    return lax.dot_general(a, b, (dims, ((), ())), preferred_element_type=F32)


def ring_order(n):
    return list(range(0, n, 2)) + list(range(n - 1 - (n % 2), 0, -2))


def ring_hop(n):
    order = ring_order(n)
    return [(order[p], order[(p + 1) % n]) for p in range(n)]


def ring_from(axis, n, step):
    order = ring_order(n)
    me = lax.axis_index(axis)
    behind = [0] * n
    for p in range(n):
        behind[order[p]] = order[(p - step) % n]
    result = jnp.int32(behind[0])
    for i in range(1, n):
        result = jnp.where(me == i, behind[i], result)
    return result


def ring_gather(value, axis, n):
    pieces = [value]
    for _ in range(n - 1):
        pieces.append(lax.ppermute(pieces[-1], axis, ring_hop(n)))
    return pieces


def local_of(block, per_device):
    return lax.div(block, jnp.int32(per_device))


def owner_walk(me, ref, live, groups, per_device, visit):
    total = jnp.int32(0)
    for kk in range(groups):
        source = me ^ kk
        alive = live[source]
        rank = jnp.int32(0)
        for k in range(SLOTS):
            hit = (k < alive) & (local_of(ref[source, k], per_device) == me)

            @pl.when(hit)
            def _(source=source, k=k, total=total, rank=rank, kk=kk):
                visit(kk, source, k, total, rank)

            step = hit.astype(jnp.int32)
            total = total + step
            rank = rank + step
    return total


def tensor_index():
    return lax.axis_index("x") * lax.axis_size("core") + lax.axis_index("core")


def pack_kernel(groups, per_device, inb, outb, live, w, packed, count):
    me = tensor_index()
    for g in range(groups):
        count[g] = 0
    alive = live[me]

    def body(k, carry):
        to = me ^ local_of(outb[me, k], per_device)

        @pl.when(k < alive)
        def _():
            packed[to, count[to]] = w[k]
            count[to] = count[to] + 1

        return carry

    lax.fori_loop(0, SLOTS, body, 0)


def compact_kernel(groups, per_device, inb, outb, live, *refs):
    pieces, out = refs[:groups], refs[groups]
    me = tensor_index()

    def visit(kk, source, k, total, rank):
        out[total] = pieces[kk][rank]

    owner_walk(me, outb, live, groups, per_device, visit)


def expand_kernel(groups, per_device, inb, outb, live, grads, packed):
    me = tensor_index()

    def visit(kk, source, k, total, rank):
        packed[kk, rank] = grads[total]

    owner_walk(me, outb, live, groups, per_device, visit)


def return_kernel(groups, per_device, inb, outb, live, *refs):
    pieces, out, count = refs[:groups], refs[groups], refs[groups + 1]
    me = tensor_index()
    for g in range(groups):
        count[g] = 0
    alive = live[me]

    def body(k, carry):
        to = me ^ local_of(outb[me, k], per_device)

        @pl.when(k < alive)
        def _():
            for g in range(groups):

                @pl.when(to == g)
                def _(g=g):
                    out[k] = pieces[g][count[g]].astype(F32)

            count[to] = count[to] + 1

        @pl.when(k >= alive)
        def _():
            out[k] = jnp.zeros(out.shape[1:], F32)

        return carry

    lax.fori_loop(0, SLOTS, body, 0)


def bottom_kernel(dense, weight, bias, cot, start, low, slope, bias_sum):
    pre = jnp.dot(dense[...], weight[...], preferred_element_type=F32) + bias[...]
    sigma = 1.0 / (1.0 + jnp.exp(-pre))
    begin = (pre * sigma).astype(BF)
    start[0] = begin
    grad = cot[...].astype(F32) * begin.astype(F32)
    low[0] = grad.astype(BF)
    slope[0] = sigma * (1.0 + pre * (1.0 - sigma))
    bias_sum[...] = jnp.sum(grad, axis=0, keepdims=True)


def fetch_inputs(groups, per_device, inb, outb, live, pieces, sbuf, tin, tout, sem):
    me = tensor_index()

    def visit(kk, source, k, total, rank):
        block = inb[source, k]
        owner = local_of(block, per_device)
        tin[total] = block + ((me ^ owner) - owner) * per_device
        tout[total] = outb[source, k] - me * per_device

    total = owner_walk(me, outb, live, groups, per_device, visit)

    def issue(j, carry):
        which = local_of(tin[j], per_device)
        col = tin[j] - which * per_device
        for g in range(groups):

            @pl.when(which == g)
            def _(g=g):
                pltpu.make_async_copy(pieces[g].at[col], sbuf.at[j], sem.at[j]).start()

        return carry

    lax.fori_loop(0, total, issue, 0)
    return total


def wait_input(pieces, sbuf, sem, j):
    pltpu.make_async_copy(pieces[0].at[0], sbuf.at[j], sem.at[j]).wait()


def block_grad_kernel(groups, per_device, ny, inb, outb, live, *refs):
    pieces = refs[:groups]
    low, out, sbuf, tmp, tin, tout, sem = refs[groups:]
    total = fetch_inputs(groups, per_device, inb, outb, live, pieces, sbuf, tin, tout, sem)
    rows = out.shape[2]

    def body(j, carry):
        wait_input(pieces, sbuf, sem, j)
        tmp[...] = dot(sbuf[j], low[tout[j]], ((0,), (0,))).astype(BF)
        for d in range(out.shape[0]):
            out[d, j] = tmp[d * rows : (d + 1) * rows, :]
        return carry

    lax.fori_loop(0, total, body, 0)


def cross_kernel(groups, per_device, nx, nz, ny, inb, outb, live, *refs):
    pieces = refs[:groups]
    low, start, cot, bias = refs[groups : groups + 4]
    shards = refs[groups + 4 : groups + 4 + nz * ny]
    cross, base, back_same, back_other = refs[groups + 4 + nz * ny : groups + 8 + nz * ny]
    wbuf, sbuf, mixed, acc, tin, tout, sem, wsem = refs[groups + 8 + nz * ny :]
    rows = shards[0].shape[1]
    copies = []
    for sz in range(nz):
        for sy in range(ny):
            d = ring_from("z", nz, sz) * ny + ring_from("y", ny, sy)
            place = pl.ds(pl.multiple_of(d * rows, rows), rows)
            copies.append(
                pltpu.make_async_copy(
                    shards[sz * ny + sy], wbuf.at[:, place, :], wsem.at[sz * ny + sy]
                )
            )
    for copy in copies:
        copy.start()
    total = fetch_inputs(groups, per_device, inb, outb, live, pieces, sbuf, tin, tout, sem)

    def clear(i, carry):
        acc[i] = jnp.zeros(acc.shape[1:], F32)
        return carry

    lax.fori_loop(0, acc.shape[0], clear, 0)

    def begin(b, carry):
        mixed[b] = jnp.broadcast_to(bias[b], mixed.shape[1:])
        return carry

    lax.fori_loop(0, per_device, begin, 0)
    for copy in copies:
        copy.wait()

    def body(j, carry):
        wait_input(pieces, sbuf, sem, j)
        part = dot(sbuf[j], wbuf[j], ((1,), (0,))).astype(BF).astype(F32)
        mixed[tout[j]] = mixed[tout[j]] + part
        back = dot(low[tout[j]], wbuf[j], ((1,), (1,))).astype(BF).astype(F32)
        acc[tin[j]] = acc[tin[j]] + back
        return carry

    lax.fori_loop(0, total, body, 0)
    for b in range(per_device):
        wide = start[b].astype(F32)
        mix = mixed[b]
        c = cot[:, b * BLK : (b + 1) * BLK].astype(F32)
        cross[:, b * BLK : (b + 1) * BLK] = (wide * mix + wide).astype(BF)
        base[b] = c * mix + c + acc[b]

    mx, core = lax.axis_index("x"), lax.axis_index("core")
    for sx in range(nx):
        rel = (mx ^ ring_from("x", nx, sx)) * 2

        def spill(b, carry, sx=sx, rel=rel):
            if sx > 0:
                back_same[sx - 1, b] = acc[rel * per_device + b].astype(BF)
            back_other[sx, b] = acc[(rel + 1) * per_device + b].astype(BF)
            return carry

        lax.fori_loop(0, per_device, spill, 0)


def pre_kernel(base, here, far, slope, low, bias_sum):
    grad = base[0] + here[0].astype(F32) + far[0].astype(F32)
    grad = grad * slope[0]
    low[0] = grad.astype(BF)
    bias_sum[...] = jnp.sum(grad, axis=0, keepdims=True)


def weight_grad_kernel(nz, ny, rows, *refs):
    grads, dense = refs[:nz], refs[nz : 2 * nz]
    own, send = refs[2 * nz :]
    for sy in range(ny):
        y = ring_from("y", ny, sy)
        cols = pl.ds(pl.multiple_of(y * rows, rows), rows)
        total = None
        for s in range(nz):
            term = dot(dense[s][:, cols], grads[s][0], ((0,), (0,)))
            total = term if total is None else total + term
        if sy == 0:
            own[...] = total
        else:
            send[sy - 1] = total.astype(BF)


def final_kernel(chunks, width, *refs):
    own, far, out = refs[:chunks], refs[chunks : 2 * chunks], refs[2 * chunks]
    for c in range(chunks):
        out[:, c * width : (c + 1) * width] = own[c][...] + far[c][...].astype(F32)


def on_device(sizes, *args):
    dense, bottom_weight, bottom_bias, cross_blocks, cross_bias, cotangent, inb, outb, live = args
    nz, ny, nx = sizes
    groups = nx * 2
    row_count, depth = dense.shape
    local_width = bottom_weight.shape[1]
    per_device = local_width // BLK
    capacity = -(-SLOTS // groups)
    width = groups * capacity
    rows = cross_blocks.shape[1]
    n_dp = nz * ny
    out_rows = depth // n_dp
    smem = pltpu.SMEM
    tables = (inb, outb, live)
    sds = jax.ShapeDtypeStruct

    def table_call(kernel, n_in, out_shape, scratch=(), in_specs=None, out_specs=None):
        single = not isinstance(out_shape, (tuple, list))
        return pl.pallas_call(
            kernel,
            out_shape=out_shape,
            grid_spec=pltpu.PrefetchScalarGridSpec(
                num_scalar_prefetch=3,
                grid=(),
                in_specs=in_specs or [VMEM] * n_in,
                out_specs=out_specs or (VMEM if single else [VMEM] * len(out_shape)),
                scratch_shapes=list(scratch),
            ),
            compiler_params=params(),
        )

    def swap(value, kk):
        return lax.ppermute(value, ("x", "core"), [(i, i ^ kk) for i in range(groups)])

    packed = table_call(
        functools.partial(pack_kernel, groups, per_device),
        1,
        sds((groups, capacity, rows, BLK), BF),
        [pltpu.SMEM((groups,), jnp.int32)],
    )(*tables, cross_blocks)
    moved = [packed[0]] + [swap(packed[kk], kk) for kk in range(1, groups)]
    shard = table_call(
        functools.partial(compact_kernel, groups, per_device),
        groups,
        sds((width, rows, BLK), BF),
    )(*tables, *moved)

    block = lambda dtype: pl.BlockSpec((1, row_count, BLK), lambda i: (i, 0, 0))
    line = pl.BlockSpec((1, BLK), lambda i: (0, i))
    wide = sds((per_device, row_count, BLK), F32)
    narrow = sds((per_device, row_count, BLK), BF)
    start, low, slope, bias_mixed = pl.pallas_call(
        bottom_kernel,
        grid=(per_device,),
        in_specs=[
            pl.BlockSpec((row_count, depth), lambda i: (0, 0)),
            pl.BlockSpec((depth, BLK), lambda i: (0, i)),
            line,
            pl.BlockSpec((row_count, BLK), lambda i: (0, i)),
        ],
        out_specs=[block(BF), block(BF), block(F32), line],
        out_shape=[narrow, narrow, wide, sds((1, local_width), F32)],
        compiler_params=params(("arbitrary",)),
    )(dense, bottom_weight, bottom_bias.reshape(1, -1), cotangent)

    if nx == 2:
        far = lax.ppermute(start, "x", [(0, 1), (1, 0)])
        flip = [(0, 1), (1, 0)]
        pieces = [start, lax.ppermute(start, "core", flip), far, lax.ppermute(far, "core", flip)]
    else:
        pieces = [start] + [swap(start, kk) for kk in range(1, groups)]

    shards = []
    for piece in ring_gather(shard, "z", nz):
        shards += ring_gather(piece, "y", ny)

    tabs = [smem((width,), jnp.int32), smem((width,), jnp.int32), pltpu.SemaphoreType.DMA((width,))]
    sbuf = pltpu.VMEM((width, row_count, BLK), BF)
    block_grads = table_call(
        functools.partial(block_grad_kernel, groups, per_device, ny),
        groups + 1,
        sds((n_dp, width, rows, BLK), BF),
        [sbuf, pltpu.VMEM((BLK, BLK), BF)] + tabs,
        in_specs=[ANY] * groups + [VMEM],
    )(*tables, *pieces, low)
    summed = lax.psum_scatter(block_grads, ("z", "y"), scatter_dimension=0, tiled=True)
    summed = summed.reshape(width, rows, BLK)
    returned = table_call(
        functools.partial(expand_kernel, groups, per_device),
        1,
        sds((groups, capacity, rows, BLK), BF),
    )(*tables, summed)
    returned = [returned[0]] + [swap(returned[kk], kk) for kk in range(1, groups)]
    grad_blocks = table_call(
        functools.partial(return_kernel, groups, per_device),
        groups,
        sds((SLOTS, rows, BLK), F32),
        [pltpu.SMEM((groups,), jnp.int32)],
    )(*tables, *returned)

    cross_out, base, back_same, back_other = table_call(
        functools.partial(cross_kernel, groups, per_device, nx, nz, ny),
        groups + 4 + n_dp,
        [
            sds((row_count, local_width), BF),
            wide,
            sds((nx - 1, per_device, row_count, BLK), BF),
            sds((nx, per_device, row_count, BLK), BF),
        ],
        [
            pltpu.VMEM((width, BLK, BLK), BF),
            sbuf,
            pltpu.VMEM((per_device, row_count, BLK), F32),
            pltpu.VMEM((groups * per_device, row_count, BLK), F32),
        ]
        + tabs
        + [pltpu.SemaphoreType.DMA((n_dp,))],
        in_specs=[ANY] * groups + [VMEM] * 4 + [ANY] * n_dp,
    )(*tables, *pieces, low, start, cotangent, cross_bias.reshape(per_device, 1, BLK), *shards)
    across = lax.ppermute(back_other, "core", [(0, 1), (1, 0)])

    plane = ny * out_rows
    order = ring_order(nz)
    dense_parts = []
    for s in range(nz):
        ahead = ring_from("z", nz, -s)
        cut = lax.dynamic_slice_in_dim(dense, ahead * plane, plane, 1)
        if s > 0:
            cut = lax.ppermute(cut, "z", [(order[p], order[(p + s) % nz]) for p in range(nz)])
        dense_parts.append(cut)

    chunks = 2 if per_device % 2 == 0 else 1
    span = per_device // chunks
    owns, fars, sums = [], [], []
    for c in range(chunks):
        sl = slice(c * span, (c + 1) * span)
        carried = None
        for sx in range(1, nx):
            term = back_same[sx - 1, sl].astype(F32) + across[sx, sl].astype(F32)
            if carried is not None:
                term = term + carried.astype(F32)
            carried = lax.ppermute(term.astype(BF), "x", ring_hop(nx))
        first = c * span
        shifted = pl.BlockSpec((1, row_count, BLK), lambda i: (i + first, 0, 0))
        plain = pl.BlockSpec((1, row_count, BLK), lambda i: (i, 0, 0))
        grad_low, sum_c = pl.pallas_call(
            pre_kernel,
            grid=(span,),
            in_specs=[shifted, shifted, plain, shifted],
            out_specs=[plain, line],
            out_shape=[sds((span, row_count, BLK), BF), sds((1, span * BLK), F32)],
            compiler_params=params(("arbitrary",)),
        )(base, across[0], carried, slope)
        sums.append(sum_c)
        gathered = ring_gather(grad_low, "z", nz)
        own, send = pl.pallas_call(
            functools.partial(weight_grad_kernel, nz, ny, out_rows),
            grid=(span,),
            in_specs=[plain] * nz + [pl.BlockSpec((row_count, plane), lambda i: (0, 0))] * nz,
            out_specs=[
                pl.BlockSpec((out_rows, BLK), lambda i: (0, i)),
                pl.BlockSpec((ny - 1, out_rows, BLK), lambda i: (0, 0, i)),
            ],
            out_shape=[
                sds((out_rows, span * BLK), F32),
                sds((ny - 1, out_rows, span * BLK), BF),
            ],
            compiler_params=params(("arbitrary",)),
        )(*gathered, *dense_parts)
        carried = None
        for sy in range(1, ny):
            term = send[sy - 1]
            if carried is not None:
                term = (term.astype(F32) + carried.astype(F32)).astype(BF)
            carried = lax.ppermute(term, "y", ring_hop(ny))
        owns.append(own)
        fars.append(carried)
    grad_bottom = pl.pallas_call(
        functools.partial(final_kernel, chunks, span * BLK),
        in_specs=[VMEM] * (2 * chunks),
        out_specs=VMEM,
        out_shape=sds((out_rows, local_width), F32),
        compiler_params=params(),
    )(*owns, *fars)

    bias = jnp.concatenate([bias_mixed] + sums, axis=1)
    for piece in ring_gather(bias, "z", nz)[1:]:
        bias = bias + piece
    for piece in ring_gather(bias, "y", ny)[1:]:
        bias = bias + piece
    bias = bias.reshape(2, local_width)
    return cross_out, grad_bottom, bias[1], grad_blocks, bias[0]


def solution(mesh):
    n_dp, groups = mesh.devices.shape
    nx = groups // 2
    ny = nx if n_dp % nx == 0 else 1
    nz = n_dp // ny
    fine = Mesh(mesh.devices.reshape(nz, ny, nx, 2), ("z", "y", "x", "core"))
    dp, tensor = ("z", "y"), ("x", "core")
    return jax.shard_map(
        functools.partial(on_device, (nz, ny, nx)),
        mesh=fine,
        in_specs=(
            P(dp, None),
            P(None, tensor),
            P(tensor),
            P(tensor, dp, None),
            P(tensor),
            P(dp, tensor),
            P(),
            P(),
            P(),
        ),
        out_specs=(
            P(dp, tensor),
            P(dp, tensor),
            P(tensor),
            P(tensor, dp, None),
            P(tensor),
        ),
        check_vma=False,
    )
```

time: 620 us -> 500 us (0.81)
  local copies, waits for them, and re-layouts: 92.3 us -> 15.4 us
  Pallas kernels: 0 us -> 73.6 us
  waiting for transfers between devices: 406 us -> 346 us
  matrix products: 46 us -> 0 us
  starting transfers between devices: 9.65 us -> 48.6 us
  blocking collectives: 36.6 us -> 0 us
  other arithmetic: 14.3 us -> 1.93 us
    ppermute x0 -> x34, waiting for transfers between devices: none -> 346 us  [the longest x17 196 us: ring_gather(): pieces.append(lax.ppermute(pieces[-1], axis, ring_hop(n)))]
    reduce_scatter x2 -> x1, waiting for transfers between devices: 242 us -> 0.01 us  [on_device(): lax.psum_scatter(block_grads, ('z', 'y'), scatter_dimension=0, tiled=True)]
    all_gather x3 -> x0, waiting for transfers between devices: 149 us -> none  [the longest x1 63.9 us: on_device(): lax.all_gather(cross_blocks, 'dp', axis=1, tiled=True)]
    pallas_call x0 -> x12, Pallas kernels: none -> 73.6 us  [the longest x1 14.2 us: on_device(): table_call(functools.partial(cross_kernel, groups, per_device, nx, nz, ny...]
    ppermute x0 -> x34, starting transfers between devices: none -> 48.6 us  [the longest x17 33.6 us: ring_gather(): pieces.append(lax.ppermute(pieces[-1], axis, ring_hop(n)))]
    dot_general x7 -> x0, matrix products: 46 us -> none  [the longest x1 12.6 us: on_device(): jnp.dot(dense, bottom_weight, preferred_element_type=jnp.float32)]
    reshape x10 -> x0, local copies, waits for them, and re-layouts: 43.8 us -> none  [the longest x4 19.5 us: pack_parts(): picked.reshape(parts.shape[0], chosen.shape[0], chosen.shape[1] * parts.s...]
    psum x1 -> x0, blocking collectives: 36.6 us -> none  [on_device(): lax.psum((jnp.sum(grad_pre, axis=0), jnp.sum(grad_mixed, axis=0)), 'dp')]
  transfers between devices with their start and end apart: 7 -> 35, of which waited for: 6 -> 23; matrix products, arithmetic and copies ran while one was open for 22% -> 2% of each run, Pallas kernels for 0% -> 10%
where the time goes in v1:
time: 500 us
  waiting for transfers between devices  346 us (69%)
  Pallas kernels  73.6 us (15%)
  starting transfers between devices  48.6 us (10%)
  local copies, waits for them, and re-layouts  15.4 us (3%)
  between operations  14.2 us (3%)
    ppermute x17, waiting for transfers between devices, ring_gather(): pieces.append(lax.ppermute(pieces[-1], axis, ring_hop(n)))  196 us
    ppermute x3, waiting for transfers between devices, on_device(): lax.ppermute(cut, 'z', [(order[p], order[(p + s) % nz]) for p in range(nz)])  41.8 us
    ppermute x1, waiting for transfers between devices, on_device(): far = lax.ppermute(start, 'x', [(0, 1), (1, 0)])  34.6 us
    ppermute x17, starting transfers between devices, ring_gather(): pieces.append(lax.ppermute(pieces[-1], axis, ring_hop(n)))  33.6 us
    ppermute x2, waiting for transfers between devices, on_device(): carried = lax.ppermute(term, 'y', ring_hop(ny))  31.3 us
    ppermute x2, waiting for transfers between devices, on_device(): carried = lax.ppermute(term.astype(BF), 'x', ring_hop(nx))  23.7 us
    pallas_call x1, Pallas kernels, on_device(): table_call(functools.partial(cross_kernel, groups, per_device, nx, nz, ny...  14.2 us
    pallas_call x1, Pallas kernels, on_device(): pl.pallas_call(bottom_kernel, grid=(per_device,), in_specs=[pl.BlockSpec(...  13.2 us
  transfers between devices with their start and end apart: 35, of which 23 were waited for; matrix products, arithmetic and copies ran while one was open for 2% of the time, Pallas kernels for 10%

profile of v1, /device:TPU:0, one launch (start us, length us, event | category | flops | bytes accessed | tf_op | source)
XLA Modules:
  0.0 499.8 jit_solution(8031047228358098445)
XLA Ops:
  7.2 13.2 %shard_map.128 = (bf16[8,192,512]{2,1,0:T(8,128)(2,1)}, bf16[8,192,512]{2,1,0:T(8,128)(2,1)}, f32[8,192,512]{2,1,0:T(8,128)}, f32[1,4096]{1,0:T(1,128)}) custom-call(bf16[192,2048]{1,0:T(8,128)(2,1)} %dense.1, bf16[2048,4096]{1,0:T(8,128)(2,1)} %weight.1, f32[1,4096]{1,0:T(1,128)} %bitcast.33, bf16[192,4096]{1,0:T(8,128)(2,1)} %refs_6_.1), custom_call_target="tpu_custom_call" | custom-call | tf_op jit(solution)/shard_map/pallas_call | solution.py:351
  20.4 2.9 collective-permute-start.1
  23.3 34.6 %collective-permute-done.1.refs_2_ = bf16[8,192,512]{2,1,0:T(8,128)(2,1)S(1)} collective-permute-done((bf16[8,192,512]{2,1,0:T(8,128)(2,1)}, bf16[8,192,512]{2,1,0:T(8,128)(2,1)S(1)}, u32[]{:S(2)}, u32[]{:S(2)}) %collective-permute-start.1) | collective-permute-done | bytes 1572896 | tf_op jit(solution)/shard_map/ppermute | solution.py:366
  57.9 3.4 collective-permute-done.2.refs_3_
  62.5 8.1 %shard_map.137 = bf16[8,12,64,512]{3,2,1,0:T(8,128)(2,1)} custom-call(s32[4,10]{1,0:T(4,128)} %inb.11, s32[4,10]{1,0:T(4,128)} %outb.11, s32[4]{0:T(128)} %live.11, bf16[8,192,512]{2,1,0:T(8,128)(2,1)} %get-tuple-element.21.refs_0_.refs_5_, bf16[8,192,512]{2,1,0:T(8,128)(2,1)} %copy-done.1, bf16[8,192,512]{2,1,0:T(8,128)(2,1)} %copy-done, ...), custom_call_target="tpu_custom_call" | custom-call | tf_op jit(solution)/shard_map/pallas_call | solution.py:378
  70.6 2.9 shard_map.129
  73.5 1.9 slice_bitcast_fusion.5
  77.4 5.9 %collective-permute-done.4.refs_2_ = bf16[3,64,512]{2,1,0:T(8,128)(2,1)S(1)} collective-permute-done((bf16[3,64,512]{2,1,0:T(8,128)(2,1)S(1)}, bf16[3,64,512]{2,1,0:T(8,128)(2,1)S(1)}, u32[]{:S(2)}, u32[]{:S(2)}) %collective-permute-start.4) | collective-permute-done | bytes 196640 | tf_op jit(solution)/shard_map/ppermute | solution.py:332
  83.3 3.2 collective-permute-done.5.refs_3_
  87.2 3.3 shard_map.130.refs_8_
  90.5 2.9 collective-permute-start.7
  93.4 44.8 %collective-permute-done.7.refs_10_ = bf16[12,64,512]{2,1,0:T(8,128)(2,1)S(1)} collective-permute-done((bf16[12,64,512]{2,1,0:T(8,128)(2,1)}, bf16[12,64,512]{2,1,0:T(8,128)(2,1)S(1)}, u32[]{:S(2)}, u32[]{:S(2)}) %collective-permute-start.7) | collective-permute-done | bytes 786464 | tf_op jit(solution)/shard_map/ppermute | solution.py:52
  138.2 27.6 %collective-permute-done.9.refs_12_ = bf16[12,64,512]{2,1,0:T(8,128)(2,1)S(1)} collective-permute-done((bf16[12,64,512]{2,1,0:T(8,128)(2,1)S(1)}, bf16[12,64,512]{2,1,0:T(8,128)(2,1)S(1)}, u32[]{:S(2)}, u32[]{:S(2)}) %collective-permute-start.9) | collective-permute-done | bytes 786464 | tf_op jit(solution)/shard_map/ppermute | solution.py:52
  170.7 15.2 %collective-permute-done.11.refs_14_ = bf16[12,64,512]{2,1,0:T(8,128)(2,1)S(1)} collective-permute-done((bf16[12,64,512]{2,1,0:T(8,128)(2,1)S(1)}, bf16[12,64,512]{2,1,0:T(8,128)(2,1)S(1)}, u32[]{:S(2)}, u32[]{:S(2)}) %collective-permute-start.11) | collective-permute-done | bytes 786464 | tf_op jit(solution)/shard_map/ppermute | solution.py:52
  187.4 3.7 collective-permute-done.6.refs_9_
  191.2 25.3 %collective-permute-done.8.refs_11_ = bf16[12,64,512]{2,1,0:T(8,128)(2,1)S(1)} collective-permute-done((bf16[12,64,512]{2,1,0:T(8,128)(2,1)S(1)}, bf16[12,64,512]{2,1,0:T(8,128)(2,1)S(1)}, u32[]{:S(2)}, u32[]{:S(2)}) %collective-permute-start.8) | collective-permute-done | bytes 786464 | tf_op jit(solution)/shard_map/ppermute | solution.py:52
  216.4 16.9 %collective-permute-done.10.refs_13_ = bf16[12,64,512]{2,1,0:T(8,128)(2,1)S(1)} collective-permute-done((bf16[12,64,512]{2,1,0:T(8,128)(2,1)S(1)}, bf16[12,64,512]{2,1,0:T(8,128)(2,1)S(1)}, u32[]{:S(2)}, u32[]{:S(2)}) %collective-permute-start.10) | collective-permute-done | bytes 786464 | tf_op jit(solution)/shard_map/ppermute | solution.py:52
  233.3 16.4 %collective-permute-done.12.refs_15_ = bf16[12,64,512]{2,1,0:T(8,128)(2,1)S(1)} collective-permute-done((bf16[12,64,512]{2,1,0:T(8,128)(2,1)S(1)}, bf16[12,64,512]{2,1,0:T(8,128)(2,1)S(1)}, u32[]{:S(2)}, u32[]{:S(2)}) %collective-permute-start.12) | collective-permute-done | bytes 786464 | tf_op jit(solution)/shard_map/ppermute | solution.py:52
  250.6 14.2 %shard_map.131 = (bf16[192,4096]{1,0:T(8,128)(2,1)}, f32[8,192,512]{2,1,0:T(8,128)}, bf16[1,8,192,512]{3,2,1,0:T(8,128)(2,1)}, bf16[2,8,192,512]{3,2,1,0:T(8,128)(2,1)}) custom-call(s32[4,10]{1,0:T(4,128)} %inb.11, s32[4,10]{1,0:T(4,128)} %outb.11, s32[4]{0:T(128)} %live.11, bf16[8,192,512]{2,1,0:T(8,128)(2,1)} %get-tuple-element.21.refs_0_.refs_5_, ...), custom_call_target="tpu_custom_call" | custom-call | tf_op jit(solution)/shard_map/pallas_call | solution.py:400
  264.9 5.9 %collective-permute-done.13 = bf16[2,8,192,512]{3,2,1,0:T(8,128)(2,1)S(1)} collective-permute-done((bf16[2,8,192,512]{3,2,1,0:T(8,128)(2,1)}, bf16[2,8,192,512]{3,2,1,0:T(8,128)(2,1)S(1)}, u32[]{:S(2)}, u32[]{:S(2)}) %collective-permute-start.13) | collective-permute-done | bytes 3145760 | tf_op jit(solution)/shard_map/ppermute | solution.py:419
  270.8 1.8 fusion.1
  272.6 1.7 collective-permute-start.21
  276.1 17.0 %collective-permute-done.21.far = bf16[4,192,512]{2,1,0:T(8,128)(2,1)S(1)} collective-permute-done((bf16[4,192,512]{2,1,0:T(8,128)(2,1)S(1)}, bf16[4,192,512]{2,1,0:T(8,128)(2,1)S(1)}, u32[]{:S(2)}, u32[]{:S(2)}) %collective-permute-start.21) | collective-permute-done | bytes 786464 | tf_op jit(solution)/shard_map/ppermute | solution.py:441
  294.0 4.1 shard_map.134
  298.1 4.3 collective-permute-start.22
  302.4 6.7 %collective-permute-done.14.far = bf16[4,192,512]{2,1,0:T(8,128)(2,1)S(1)} collective-permute-done((bf16[4,192,512]{2,1,0:T(8,128)(2,1)S(1)}, bf16[4,192,512]{2,1,0:T(8,128)(2,1)S(1)}, u32[]{:S(2)}, u32[]{:S(2)}) %collective-permute-start.14) | collective-permute-done | bytes 786464 | tf_op jit(solution)/shard_map/ppermute | solution.py:441
  310.0 4.1 shard_map.132
  314.1 4.3 collective-permute-start.15
  318.4 3.1 collective-permute-start.23
  321.5 15.2 %collective-permute-done.15.refs_1_ = bf16[4,192,512]{2,1,0:T(8,128)(2,1)S(1)} collective-permute-done((bf16[4,192,512]{2,1,0:T(8,128)(2,1)}, bf16[4,192,512]{2,1,0:T(8,128)(2,1)S(1)}, u32[]{:S(2)}, u32[]{:S(2)}) %collective-permute-start.15) | collective-permute-done | bytes 786464 | tf_op jit(solution)/shard_map/ppermute | solution.py:52
  336.7 3.3 collective-permute-start.16
  340.8 28.6 %collective-permute-done.27 = f32[1,8192]{1,0:T(1,128)S(1)} collective-permute-done((f32[1,8192]{1,0:T(1,128)S(1)}, f32[1,8192]{1,0:T(1,128)S(1)}, u32[]{:S(2)}, u32[]{:S(2)}) %collective-permute-start.27) | collective-permute-done | bytes 32800 | tf_op jit(solution)/shard_map/ppermute | solution.py:52
  369.4 3.4 collective-permute-start.28
  374.4 3.2 collective-permute-start.29
  379.5 1.7 collective-permute-start.30
  382.0 3.4 collective-permute-start.18
  386.0 31.8 %collective-permute-done.18.refs_5_ = bf16[192,512]{1,0:T(8,128)(2,1)S(1)} collective-permute-done((bf16[192,512]{1,0:T(8,128)(2,1)S(1)}, bf16[192,512]{1,0:T(8,128)(2,1)S(1)}, u32[]{:S(2)}, u32[]{:S(2)}) %collective-permute-start.18) | collective-permute-done | bytes 196640 | tf_op jit(solution)/shard_map/ppermute | solution.py:428
  417.8 3.8 collective-permute-done.19.refs_6_
  421.6 6.2 %collective-permute-done.20.refs_7_ = bf16[192,512]{1,0:T(8,128)(2,1)S(1)} collective-permute-done((bf16[192,512]{1,0:T(8,128)(2,1)S(1)}, bf16[192,512]{1,0:T(8,128)(2,1)S(1)}, u32[]{:S(2)}, u32[]{:S(2)}) %collective-permute-start.20) | collective-permute-done | bytes 196640 | tf_op jit(solution)/shard_map/ppermute | solution.py:428
  428.8 5.9 %shard_map.135 = (f32[256,2048]{1,0:T(8,128)}, bf16[1,256,2048]{2,1,0:T(8,128)(2,1)}) custom-call(bf16[4,192,512]{2,1,0:T(8,128)(2,1)} %get-tuple-element.30.refs_0_, bf16[4,192,512]{2,1,0:T(8,128)(2,1)} %copy-done.15, bf16[4,192,512]{2,1,0:T(8,128)(2,1)} %collective-permute-done.23.refs_2_, bf16[4,192,512]{2,1,0:T(8,128)(2,1)} %copy-done.19, ...), custom_call_target="tpu_custom_call" | custom-call | tf_op jit(solution)/shard_map/pallas_call | solution.py:455
  434.7 1.8 collective-permute-start.26
  437.3 5.9 %shard_map.133 = (f32[256,2048]{1,0:T(8,128)}, bf16[1,256,2048]{2,1,0:T(8,128)(2,1)}) custom-call(bf16[4,192,512]{2,1,0:T(8,128)(2,1)} %get-tuple-element.28.refs_0_, bf16[4,192,512]{2,1,0:T(8,128)(2,1)} %copy-done.16, bf16[4,192,512]{2,1,0:T(8,128)(2,1)} %copy-done.17, bf16[4,192,512]{2,1,0:T(8,128)(2,1)} %copy-done.18, ...), custom_call_target="tpu_custom_call" | custom-call | tf_op jit(solution)/shard_map/pallas_call | solution.py:455
  443.5 3.2 shard_map.138
  446.8 2.0 slice_bitcast_fusion.1
  451.2 9.8 %collective-permute-done.26.refs_3_ = bf16[256,2048]{1,0:T(8,128)(2,1)S(1)} collective-permute-done((bf16[256,2048]{1,0:T(8,128)(2,1)}, bf16[256,2048]{1,0:T(8,128)(2,1)S(1)}, u32[]{:S(2)}, u32[]{:S(2)}) %collective-permute-start.26) | collective-permute-done | bytes 1048608 | tf_op jit(solution)/shard_map/ppermute | solution.py:474
  461.0 21.5 %collective-permute-done.25.refs_2_ = bf16[256,2048]{1,0:T(8,128)(2,1)S(1)} collective-permute-done((bf16[256,2048]{1,0:T(8,128)(2,1)}, bf16[256,2048]{1,0:T(8,128)(2,1)S(1)}, u32[]{:S(2)}, u32[]{:S(2)}) %collective-permute-start.25) | collective-permute-done | bytes 1048608 | tf_op jit(solution)/shard_map/ppermute | solution.py:474
  483.5 5.1 %shard_map.136 = f32[256,4096]{1,0:T(8,128)} custom-call(f32[256,2048]{1,0:T(8,128)} %get-tuple-element.29.refs_0_, f32[256,2048]{1,0:T(8,128)} %get-tuple-element.31.refs_1_, bf16[256,2048]{1,0:T(8,128)(2,1)} %copy-done.5, bf16[256,2048]{1,0:T(8,128)(2,1)} %copy-done.4), custom_call_target="tpu_custom_call" | custom-call | tf_op jit(solution)/shard_map/pallas_call | solution.py:477
  489.5 3.5 shard_map.139
  (108 shorter events, 26.8 us)
Async XLA Ops:
  7.2 436.4 %reduce-scatter.2.cloned.1.call-start = ((), (), s32[]{:S(2)}) async-start(), calls=%async_computation.1 | async-start | bytes 7077888 | tf_op jit(solution)/shard_map/reduce_scatter | solution.py:385
  20.4 37.5 %collective-permute-start.1 = (bf16[8,192,512]{2,1,0:T(8,128)(2,1)}, bf16[8,192,512]{2,1,0:T(8,128)(2,1)S(1)}, u32[]{:S(2)}, u32[]{:S(2)}) collective-permute-start(bf16[8,192,512]{2,1,0:T(8,128)(2,1)} %get-tuple-element.21.refs_0_.refs_5_), channel_id=1, source_target_pairs={{0,2},{2,0},{1,3},{3,1},{4,6},{6,4},{5,7},{7,5},{8,10},{10,8},{9,1... | collective-permute-start | bytes 4718600 | tf_op jit(solution)/shard_map/ppermute | solution.py:366
  23.3 34.6 %collective-permute-start = (bf16[8,192,512]{2,1,0:T(8,128)(2,1)}, bf16[8,192,512]{2,1,0:T(8,128)(2,1)S(1)}, u32[]{:S(2)}, u32[]{:S(2)}) collective-permute-start(bf16[8,192,512]{2,1,0:T(8,128)(2,1)} %get-tuple-element.21.refs_0_.refs_5_), channel_id=1, source_target_pairs={{0,1},{1,0},{2,3},{3,2},{4,5},{5,4},{6,7},{7,6},{8,9},{9,8},{10,11... | collective-permute-start | bytes 4718600 | tf_op jit(solution)/shard_map/ppermute | solution.py:368
  57.9 3.4 collective-permute-start.2
  75.5 1.9 collective-permute-start.3
  75.6 7.7 %collective-permute-start.4 = (bf16[3,64,512]{2,1,0:T(8,128)(2,1)S(1)}, bf16[3,64,512]{2,1,0:T(8,128)(2,1)S(1)}, u32[]{:S(2)}, u32[]{:S(2)}) collective-permute-start(bf16[3,64,512]{2,1,0:T(8,128)(2,1)S(1)} %get-tuple-element.48), channel_id=1, source_target_pairs={{0,2},{1,3},{2,0},{3,1},{4,6},{5,7},{6,4},{7,5},{8,10},{9,11},{10,... | collective-permute-start | bytes 589832 | tf_op jit(solution)/shard_map/ppermute | solution.py:332
  77.2 9.3 %collective-permute-start.5 = (bf16[3,64,512]{2,1,0:T(8,128)(2,1)S(1)}, bf16[3,64,512]{2,1,0:T(8,128)(2,1)S(1)}, u32[]{:S(2)}, u32[]{:S(2)}) collective-permute-start(bf16[3,64,512]{2,1,0:T(8,128)(2,1)S(1)} %get-tuple-element.47), channel_id=1, source_target_pairs={{0,3},{1,2},{2,1},{3,0},{4,7},{5,6},{6,5},{7,4},{8,11},{9,10},{10,... | collective-permute-start | bytes 589832 | tf_op jit(solution)/shard_map/ppermute | solution.py:332
  90.5 47.7 %collective-permute-start.7 = (bf16[12,64,512]{2,1,0:T(8,128)(2,1)}, bf16[12,64,512]{2,1,0:T(8,128)(2,1)S(1)}, u32[]{:S(2)}, u32[]{:S(2)}) collective-permute-start(bf16[12,64,512]{2,1,0:T(8,128)(2,1)} %shard_map.130.refs_8_), channel_id=1, source_target_pairs={{0,16},{16,24},{24,8},{8,0},{1,17},{17,25},{25,9},{9,1},{2,18},{18... | collective-permute-start | bytes 2359304 | tf_op jit(solution)/shard_map/ppermute | solution.py:52
  138.2 111.6 %copy-start.6 = (bf16[12,64,512]{2,1,0:T(8,128)(2,1)}, bf16[12,64,512]{2,1,0:T(8,128)(2,1)S(1)}, u32[]{:S(2)}) copy-start(bf16[12,64,512]{2,1,0:T(8,128)(2,1)S(1)} %collective-permute-done.7.refs_10_) | copy-start | bytes 2359300
  138.2 27.6 %collective-permute-start.9 = (bf16[12,64,512]{2,1,0:T(8,128)(2,1)S(1)}, bf16[12,64,512]{2,1,0:T(8,128)(2,1)S(1)}, u32[]{:S(2)}, u32[]{:S(2)}) collective-permute-start(bf16[12,64,512]{2,1,0:T(8,128)(2,1)S(1)} %collective-permute-done.7.refs_10_), channel_id=1, source_target_pairs={{0,16},{16,24},{24,8},{8,0},{1,17},{17,25},{25,9},{9,1},{2,18},{18... | collective-permute-start | bytes 2359304 | tf_op jit(solution)/shard_map/ppermute | solution.py:52
  165.7 84.0 %copy-start.7 = (bf16[12,64,512]{2,1,0:T(8,128)(2,1)}, bf16[12,64,512]{2,1,0:T(8,128)(2,1)S(1)}, u32[]{:S(2)}) copy-start(bf16[12,64,512]{2,1,0:T(8,128)(2,1)S(1)} %collective-permute-done.9.refs_12_) | copy-start | bytes 2359300
  165.7 20.2 %collective-permute-start.11 = (bf16[12,64,512]{2,1,0:T(8,128)(2,1)S(1)}, bf16[12,64,512]{2,1,0:T(8,128)(2,1)S(1)}, u32[]{:S(2)}, u32[]{:S(2)}) collective-permute-start(bf16[12,64,512]{2,1,0:T(8,128)(2,1)S(1)} %collective-permute-done.9.refs_12_), channel_id=1, source_target_pairs={{0,16},{16,24},{24,8},{8,0},{1,17},{17,25},{25,9},{9,1},{2,18},{18... | collective-permute-start | bytes 2359304 | tf_op jit(solution)/shard_map/ppermute | solution.py:52
  167.1 24.1 %collective-permute-start.6 = (bf16[12,64,512]{2,1,0:T(8,128)(2,1)}, bf16[12,64,512]{2,1,0:T(8,128)(2,1)S(1)}, u32[]{:S(2)}, u32[]{:S(2)}) collective-permute-start(bf16[12,64,512]{2,1,0:T(8,128)(2,1)} %shard_map.130.refs_8_), channel_id=1, source_target_pairs={{0,4},{4,0},{1,5},{5,1},{2,6},{6,2},{3,7},{7,3},{8,12},{12,8},{9,1... | collective-permute-start | bytes 2359304 | tf_op jit(solution)/shard_map/ppermute | solution.py:52
  168.7 47.8 %collective-permute-start.8 = (bf16[12,64,512]{2,1,0:T(8,128)(2,1)S(1)}, bf16[12,64,512]{2,1,0:T(8,128)(2,1)S(1)}, u32[]{:S(2)}, u32[]{:S(2)}) collective-permute-start(bf16[12,64,512]{2,1,0:T(8,128)(2,1)S(1)} %collective-permute-done.7.refs_10_), channel_id=1, source_target_pairs={{0,4},{4,0},{1,5},{5,1},{2,6},{6,2},{3,7},{7,3},{8,12},{12,8},{9,1... | collective-permute-start | bytes 2359304 | tf_op jit(solution)/shard_map/ppermute | solution.py:52
  169.1 64.2 %collective-permute-start.10 = (bf16[12,64,512]{2,1,0:T(8,128)(2,1)S(1)}, bf16[12,64,512]{2,1,0:T(8,128)(2,1)S(1)}, u32[]{:S(2)}, u32[]{:S(2)}) collective-permute-start(bf16[12,64,512]{2,1,0:T(8,128)(2,1)S(1)} %collective-permute-done.9.refs_12_), channel_id=1, source_target_pairs={{0,4},{4,0},{1,5},{5,1},{2,6},{6,2},{3,7},{7,3},{8,12},{12,8},{9,1... | collective-permute-start | bytes 2359304 | tf_op jit(solution)/shard_map/ppermute | solution.py:52
  185.9 63.8 %copy-start.8 = (bf16[12,64,512]{2,1,0:T(8,128)(2,1)}, bf16[12,64,512]{2,1,0:T(8,128)(2,1)S(1)}, u32[]{:S(2)}) copy-start(bf16[12,64,512]{2,1,0:T(8,128)(2,1)S(1)} %collective-permute-done.11.refs_14_) | copy-start | bytes 2359300
  185.9 63.8 %collective-permute-start.12 = (bf16[12,64,512]{2,1,0:T(8,128)(2,1)S(1)}, bf16[12,64,512]{2,1,0:T(8,128)(2,1)S(1)}, u32[]{:S(2)}, u32[]{:S(2)}) collective-permute-start(bf16[12,64,512]{2,1,0:T(8,128)(2,1)S(1)} %collective-permute-done.11.refs_14_), channel_id=1, source_target_pairs={{0,4},{4,0},{1,5},{5,1},{2,6},{6,2},{3,7},{7,3},{8,12},{12,8},{9,1... | collective-permute-start | bytes 2359304 | tf_op jit(solution)/shard_map/ppermute | solution.py:52
  191.2 58.6 %copy-start.9 = (bf16[12,64,512]{2,1,0:T(8,128)(2,1)}, bf16[12,64,512]{2,1,0:T(8,128)(2,1)S(1)}, u32[]{:S(2)}) copy-start(bf16[12,64,512]{2,1,0:T(8,128)(2,1)S(1)} %collective-permute-done.6.refs_9_) | copy-start | bytes 2359300
  216.4 33.3 %copy-start.10 = (bf16[12,64,512]{2,1,0:T(8,128)(2,1)}, bf16[12,64,512]{2,1,0:T(8,128)(2,1)S(1)}, u32[]{:S(2)}) copy-start(bf16[12,64,512]{2,1,0:T(8,128)(2,1)S(1)} %collective-permute-done.8.refs_11_) | copy-start | bytes 2359300
  233.3 16.4 %copy-start.11 = (bf16[12,64,512]{2,1,0:T(8,128)(2,1)}, bf16[12,64,512]{2,1,0:T(8,128)(2,1)S(1)}, u32[]{:S(2)}) copy-start(bf16[12,64,512]{2,1,0:T(8,128)(2,1)S(1)} %collective-permute-done.10.refs_13_) | copy-start | bytes 2359300
  264.9 5.9 %collective-permute-start.13 = (bf16[2,8,192,512]{3,2,1,0:T(8,128)(2,1)}, bf16[2,8,192,512]{3,2,1,0:T(8,128)(2,1)S(1)}, u32[]{:S(2)}, u32[]{:S(2)}) collective-permute-start(bf16[2,8,192,512]{3,2,1,0:T(8,128)(2,1)} %get-tuple-element.25), channel_id=1, source_target_pairs={{0,1},{1,0},{2,3},{3,2},{4,5},{5,4},{6,7},{7,6},{8,9},{9,8},{10,11... | collective-permute-start | bytes 9437192 | tf_op jit(solution)/shard_map/ppermute | solution.py:419
  272.6 20.4 %collective-permute-start.21 = (bf16[4,192,512]{2,1,0:T(8,128)(2,1)S(1)}, bf16[4,192,512]{2,1,0:T(8,128)(2,1)S(1)}, u32[]{:S(2)}, u32[]{:S(2)}) collective-permute-start(bf16[4,192,512]{2,1,0:T(8,128)(2,1)S(1)} %get-tuple-element.37), channel_id=1, source_target_pairs={{0,2},{2,0},{1,3},{3,1},{4,6},{6,4},{5,7},{7,5},{8,10},{10,8},{9,1... | collective-permute-start | bytes 2359304 | tf_op jit(solution)/shard_map/ppermute | solution.py:441
  274.4 34.8 %collective-permute-start.14 = (bf16[4,192,512]{2,1,0:T(8,128)(2,1)S(1)}, bf16[4,192,512]{2,1,0:T(8,128)(2,1)S(1)}, u32[]{:S(2)}, u32[]{:S(2)}) collective-permute-start(bf16[4,192,512]{2,1,0:T(8,128)(2,1)S(1)} %get-tuple-element.38), channel_id=1, source_target_pairs={{0,2},{2,0},{1,3},{3,1},{4,6},{6,4},{5,7},{7,5},{8,10},{10,8},{9,1... | collective-permute-start | bytes 2359304 | tf_op jit(solution)/shard_map/ppermute | solution.py:441
  298.1 41.9 %copy-start.29 = (f32[1,4096]{1,0:T(1,128)S(1)}, f32[1,4096]{1,0:T(1,128)}, u32[]{:S(2)}) copy-start(f32[1,4096]{1,0:T(1,128)} %get-tuple-element.34) | copy-start | bytes 49156
  298.1 42.6 %copy-start.30 = (f32[1,2048]{1,0:T(1,128)S(1)}, f32[1,2048]{1,0:T(1,128)}, u32[]{:S(2)}) copy-start(f32[1,2048]{1,0:T(1,128)} %get-tuple-element.36) | copy-start | bytes 24580
  298.1 83.1 %copy-start.3 = (bf16[192,2048]{1,0:T(8,128)(2,1)S(1)}, bf16[192,2048]{1,0:T(8,128)(2,1)}, u32[]{:S(2)}) copy-start(bf16[192,2048]{1,0:T(8,128)(2,1)} %dense.1) | copy-start | bytes 2359300
  298.1 20.3 %collective-permute-start.22 = (bf16[4,192,512]{2,1,0:T(8,128)(2,1)}, bf16[4,192,512]{2,1,0:T(8,128)(2,1)S(1)}, u32[]{:S(2)}, u32[]{:S(2)}) collective-permute-start(bf16[4,192,512]{2,1,0:T(8,128)(2,1)} %get-tuple-element.30.refs_0_), channel_id=1, source_target_pairs={{0,16},{16,24},{24,8},{8,0},{1,17},{17,25},{25,9},{9,1},{2,18},{18... | collective-permute-start | bytes 2359304 | tf_op jit(solution)/shard_map/ppermute | solution.py:52
  314.1 22.6 %collective-permute-start.15 = (bf16[4,192,512]{2,1,0:T(8,128)(2,1)}, bf16[4,192,512]{2,1,0:T(8,128)(2,1)S(1)}, u32[]{:S(2)}, u32[]{:S(2)}) collective-permute-start(bf16[4,192,512]{2,1,0:T(8,128)(2,1)} %get-tuple-element.28.refs_0_), channel_id=1, source_target_pairs={{0,16},{16,24},{24,8},{8,0},{1,17},{17,25},{25,9},{9,1},{2,18},{18... | collective-permute-start | bytes 2359304 | tf_op jit(solution)/shard_map/ppermute | solution.py:52
  318.4 109.4 %copy-start.15 = (bf16[4,192,512]{2,1,0:T(8,128)(2,1)}, bf16[4,192,512]{2,1,0:T(8,128)(2,1)S(1)}, u32[]{:S(2)}) copy-start(bf16[4,192,512]{2,1,0:T(8,128)(2,1)S(1)} %collective-permute-done.22.refs_1_) | copy-start | bytes 2359300
  318.4 59.2 %collective-permute-start.23 = (bf16[4,192,512]{2,1,0:T(8,128)(2,1)S(1)}, bf16[4,192,512]{2,1,0:T(8,128)(2,1)}, u32[]{:S(2)}, u32[]{:S(2)}) collective-permute-start(bf16[4,192,512]{2,1,0:T(8,128)(2,1)S(1)} %collective-permute-done.22.refs_1_), channel_id=1, source_target_pairs={{0,16},{16,24},{24,8},{8,0},{1,17},{17,25},{25,9},{9,1},{2,18},{18... | collective-permute-start | bytes 2359304 | tf_op jit(solution)/shard_map/ppermute | solution.py:52
  336.7 97.9 %copy-start.16 = (bf16[4,192,512]{2,1,0:T(8,128)(2,1)}, bf16[4,192,512]{2,1,0:T(8,128)(2,1)S(1)}, u32[]{:S(2)}) copy-start(bf16[4,192,512]{2,1,0:T(8,128)(2,1)S(1)} %collective-permute-done.15.refs_1_) | copy-start | bytes 2359300
  336.7 40.9 %collective-permute-start.16 = (bf16[4,192,512]{2,1,0:T(8,128)(2,1)S(1)}, bf16[4,192,512]{2,1,0:T(8,128)(2,1)S(1)}, u32[]{:S(2)}, u32[]{:S(2)}) collective-permute-start(bf16[4,192,512]{2,1,0:T(8,128)(2,1)S(1)} %collective-permute-done.15.refs_1_), channel_id=1, source_target_pairs={{0,16},{16,24},{24,8},{8,0},{1,17},{17,25},{25,9},{9,1},{2,18},{18... | collective-permute-start | bytes 2359304 | tf_op jit(solution)/shard_map/ppermute | solution.py:52
  340.7 28.7 %collective-permute-start.27 = (f32[1,8192]{1,0:T(1,128)S(1)}, f32[1,8192]{1,0:T(1,128)S(1)}, u32[]{:S(2)}, u32[]{:S(2)}) collective-permute-start(f32[1,8192]{1,0:T(1,128)S(1)} %constant_dynamic-update-slice_fusion), channel_id=1, source_target_pairs={{0,16},{16,24},{24,8},{8,0},{1,17},{17,25},{25,9},{9,1},{2,18},{18... | collective-permute-start | bytes 98312 | tf_op jit(solution)/shard_map/ppermute | solution.py:52
  369.4 5.0 collective-permute-start.28
  374.4 5.1 %collective-permute-start.29 = (f32[1,8192]{1,0:T(1,128)S(1)}, f32[1,8192]{1,0:T(1,128)S(1)}, u32[]{:S(2)}, u32[]{:S(2)}) collective-permute-start(f32[1,8192]{1,0:T(1,128)S(1)} %collective-permute-done.28), channel_id=1, source_target_pairs={{0,16},{16,24},{24,8},{8,0},{1,17},{17,25},{25,9},{9,1},{2,18},{18... | collective-permute-start | bytes 98312 | tf_op jit(solution)/shard_map/ppermute | solution.py:52
  377.6 50.2 %collective-permute-start.24 = (bf16[4,192,512]{2,1,0:T(8,128)(2,1)}, bf16[4,192,512]{2,1,0:T(8,128)(2,1)S(1)}, u32[]{:S(2)}, u32[]{:S(2)}) collective-permute-start(bf16[4,192,512]{2,1,0:T(8,128)(2,1)} %collective-permute-done.23.refs_2_), channel_id=1, source_target_pairs={{0,16},{16,24},{24,8},{8,0},{1,17},{17,25},{25,9},{9,1},{2,18},{18... | collective-permute-start | bytes 2359304 | tf_op jit(solution)/shard_map/ppermute | solution.py:52
  377.6 57.0 %copy-start.17 = (bf16[4,192,512]{2,1,0:T(8,128)(2,1)}, bf16[4,192,512]{2,1,0:T(8,128)(2,1)S(1)}, u32[]{:S(2)}) copy-start(bf16[4,192,512]{2,1,0:T(8,128)(2,1)S(1)} %collective-permute-done.16.refs_2_) | copy-start | bytes 2359300
  377.6 58.8 %collective-permute-start.17 = (bf16[4,192,512]{2,1,0:T(8,128)(2,1)S(1)}, bf16[4,192,512]{2,1,0:T(8,128)(2,1)S(1)}, u32[]{:S(2)}, u32[]{:S(2)}) collective-permute-start(bf16[4,192,512]{2,1,0:T(8,128)(2,1)S(1)} %collective-permute-done.16.refs_2_), channel_id=1, source_target_pairs={{0,16},{16,24},{24,8},{8,0},{1,17},{17,25},{25,9},{9,1},{2,18},{18... | collective-permute-start | bytes 2359304 | tf_op jit(solution)/shard_map/ppermute | solution.py:52
  379.5 6.1 %collective-permute-start.30 = (f32[1,8192]{1,0:T(1,128)S(1)}, f32[1,8192]{1,0:T(1,128)S(1)}, u32[]{:S(2)}, u32[]{:S(2)}) collective-permute-start(f32[1,8192]{1,0:T(1,128)S(1)} %add_add_fusion), channel_id=1, source_target_pairs={{0,4},{4,0},{1,5},{5,1},{2,6},{6,2},{3,7},{7,3},{8,12},{12,8},{9,1... | collective-permute-start | bytes 98312 | tf_op jit(solution)/shard_map/ppermute | solution.py:52
  382.0 35.8 %collective-permute-start.18 = (bf16[192,512]{1,0:T(8,128)(2,1)S(1)}, bf16[192,512]{1,0:T(8,128)(2,1)S(1)}, u32[]{:S(2)}, u32[]{:S(2)}) collective-permute-start(bf16[192,512]{1,0:T(8,128)(2,1)S(1)} %get-tuple-element.44), channel_id=1, source_target_pairs={{0,16},{16,24},{24,8},{8,0},{1,17},{17,25},{25,9},{9,1},{2,18},{18... | collective-permute-start | bytes 589832 | tf_op jit(solution)/shard_map/ppermute | solution.py:428
  385.4 36.1 %collective-permute-start.19 = (bf16[192,512]{1,0:T(8,128)(2,1)S(1)}, bf16[192,512]{1,0:T(8,128)(2,1)S(1)}, u32[]{:S(2)}, u32[]{:S(2)}) collective-permute-start(bf16[192,512]{1,0:T(8,128)(2,1)S(1)} %get-tuple-element.46), channel_id=1, source_target_pairs={{0,24},{16,8},{24,0},{8,16},{1,25},{17,9},{25,1},{9,17},{2,26},{18... | collective-permute-start | bytes 589832 | tf_op jit(solution)/shard_map/ppermute | solution.py:428
  385.6 42.2 %collective-permute-start.20 = (bf16[192,512]{1,0:T(8,128)(2,1)S(1)}, bf16[192,512]{1,0:T(8,128)(2,1)S(1)}, u32[]{:S(2)}, u32[]{:S(2)}) collective-permute-start(bf16[192,512]{1,0:T(8,128)(2,1)S(1)} %get-tuple-element.43), channel_id=1, source_target_pairs={{0,8},{16,0},{24,16},{8,24},{1,9},{17,1},{25,17},{9,25},{2,10},{18... | collective-permute-start | bytes 589832 | tf_op jit(solution)/shard_map/ppermute | solution.py:428
  434.7 26.3 %collective-permute-start.26 = (bf16[256,2048]{1,0:T(8,128)(2,1)}, bf16[256,2048]{1,0:T(8,128)(2,1)S(1)}, u32[]{:S(2)}, u32[]{:S(2)}) collective-permute-start(bf16[256,2048]{1,0:T(8,128)(2,1)} %bitcast.34), channel_id=1, source_target_pairs={{0,4},{4,0},{1,5},{5,1},{2,6},{6,2},{3,7},{7,3},{8,12},{12,8},{9,1... | collective-permute-start | bytes 3145736 | tf_op jit(solution)/shard_map/ppermute | solution.py:474
  443.2 39.3 %collective-permute-start.25 = (bf16[256,2048]{1,0:T(8,128)(2,1)}, bf16[256,2048]{1,0:T(8,128)(2,1)S(1)}, u32[]{:S(2)}, u32[]{:S(2)}) collective-permute-start(bf16[256,2048]{1,0:T(8,128)(2,1)} %bitcast.35), channel_id=1, source_target_pairs={{0,4},{4,0},{1,5},{5,1},{2,6},{6,2},{3,7},{7,3},{8,12},{12,8},{9,1... | collective-permute-start | bytes 3145736 | tf_op jit(solution)/shard_map/ppermute | solution.py:474
  448.7 39.9 %collective-permute-start.31 = (bf16[3,64,512]{2,1,0:T(8,128)(2,1)S(1)}, bf16[3,64,512]{2,1,0:T(8,128)(2,1)S(1)}, u32[]{:S(2)}, u32[]{:S(2)}) collective-permute-start(bf16[3,64,512]{2,1,0:T(8,128)(2,1)S(1)} %get-tuple-element.41), channel_id=1, source_target_pairs={{0,1},{1,0},{2,3},{3,2},{4,5},{5,4},{6,7},{7,6},{8,9},{9,8},{10,11... | collective-permute-start | bytes 589832 | tf_op jit(solution)/shard_map/ppermute | solution.py:332
  448.7 39.9 %collective-permute-start.32 = (bf16[3,64,512]{2,1,0:T(8,128)(2,1)S(1)}, bf16[3,64,512]{2,1,0:T(8,128)(2,1)S(1)}, u32[]{:S(2)}, u32[]{:S(2)}) collective-permute-start(bf16[3,64,512]{2,1,0:T(8,128)(2,1)S(1)} %get-tuple-element.40), channel_id=1, source_target_pairs={{0,2},{1,3},{2,0},{3,1},{4,6},{5,7},{6,4},{7,5},{8,10},{9,11},{10,... | collective-permute-start | bytes 589832 | tf_op jit(solution)/shard_map/ppermute | solution.py:332
  450.4 38.2 %collective-permute-start.33 = (bf16[3,64,512]{2,1,0:T(8,128)(2,1)S(1)}, bf16[3,64,512]{2,1,0:T(8,128)(2,1)S(1)}, u32[]{:S(2)}, u32[]{:S(2)}) collective-permute-start(bf16[3,64,512]{2,1,0:T(8,128)(2,1)S(1)} %get-tuple-element.39), channel_id=1, source_target_pairs={{0,3},{1,2},{2,1},{3,0},{4,7},{5,6},{6,5},{7,4},{8,11},{9,10},{10,... | collective-permute-start | bytes 589832 | tf_op jit(solution)/shard_map/ppermute | solution.py:332
  461.0 21.5 %copy-start.4 = (bf16[256,2048]{1,0:T(8,128)(2,1)}, bf16[256,2048]{1,0:T(8,128)(2,1)S(1)}, u32[]{:S(2)}) copy-start(bf16[256,2048]{1,0:T(8,128)(2,1)S(1)} %collective-permute-done.26.refs_3_) | copy-start | bytes 3145732
  (18 other events, 45.6 us)
Sparse Core Ops, SparseCore 0:
  70.8 158.0 reduce-scatter.1

commit v2 on v1

--- a/solution.py
+++ b/solution.py
@@ -10,6 +10,7 @@
 
 BLK = 512
 SLOTS = 10
+EXTRA = 16
 BF = jnp.bfloat16
 F32 = jnp.float32
 ANY = pl.BlockSpec(memory_space=pl.ANY)
@@ -46,6 +47,10 @@
     return result
 
 
+def tie(*values):
+    return lax.optimization_barrier(tuple(values))
+
+
 def ring_gather(value, axis, n):
     pieces = [value]
     for _ in range(n - 1):
@@ -80,7 +85,8 @@
     return lax.axis_index("x") * lax.axis_size("core") + lax.axis_index("core")
 
 
-def pack_kernel(groups, per_device, inb, outb, live, w, packed, count):
+def pack_kernel(groups, per_device, inb, outb, live, w, *refs):
+    packed, count = refs[:groups], refs[groups]
     me = tensor_index()
     for g in range(groups):
         count[g] = 0
@@ -91,7 +97,12 @@
 
         @pl.when(k < alive)
         def _():
-            packed[to, count[to]] = w[k]
+            for g in range(groups):
+
+                @pl.when(to == g)
+                def _(g=g):
+                    packed[g][count[g]] = w[k]
+
             count[to] = count[to] + 1
 
         return carry
@@ -109,11 +120,11 @@
     owner_walk(me, outb, live, groups, per_device, visit)
 
 
-def expand_kernel(groups, per_device, inb, outb, live, grads, packed):
+def expand_kernel(groups, per_device, inb, outb, live, grads, *packed):
     me = tensor_index()
 
     def visit(kk, source, k, total, rank):
-        packed[kk, rank] = grads[total]
+        packed[kk][rank] = grads[total]
 
     owner_walk(me, outb, live, groups, per_device, visit)
 
@@ -268,16 +279,23 @@
         lax.fori_loop(0, per_device, spill, 0)
 
 
-def pre_kernel(base, here, far, slope, low, bias_sum):
+def pre_kernel(base, here, far, slope, low):
     grad = base[0] + here[0].astype(F32) + far[0].astype(F32)
     grad = grad * slope[0]
     low[0] = grad.astype(BF)
-    bias_sum[...] = jnp.sum(grad, axis=0, keepdims=True)
 
 
 def weight_grad_kernel(nz, ny, rows, *refs):
     grads, dense = refs[:nz], refs[nz : 2 * nz]
     own, send = refs[2 * nz :]
+    column = grads[0][0].astype(F32)
+    for s in range(1, nz):
+        column = column + grads[s][0].astype(F32)
+    column = jnp.sum(column, axis=0, keepdims=True)
+    high = column.astype(BF).astype(F32)
+    place = lax.broadcasted_iota(jnp.int32, (EXTRA, BLK), 0)
+    own[rows:, :] = jnp.where(place == 0, column, 0.0)
+    extra = jnp.where(place == 0, high, jnp.where(place == 1, column - high, 0.0)).astype(BF)
     for sy in range(ny):
         y = ring_from("y", ny, sy)
         cols = pl.ds(pl.multiple_of(y * rows, rows), rows)
@@ -286,15 +304,19 @@
             term = dot(dense[s][:, cols], grads[s][0], ((0,), (0,)))
             total = term if total is None else total + term
         if sy == 0:
-            own[...] = total
+            own[:rows, :] = total
         else:
-            send[sy - 1] = total.astype(BF)
-
-
-def final_kernel(chunks, width, *refs):
-    own, far, out = refs[:chunks], refs[chunks : 2 * chunks], refs[2 * chunks]
+            send[sy - 1, :rows, :] = total.astype(BF)
+            send[sy - 1, rows:, :] = extra
+
+
+def final_kernel(chunks, width, rows, *refs):
+    own, far, (out, bias) = refs[:chunks], refs[chunks : 2 * chunks], refs[2 * chunks :]
     for c in range(chunks):
-        out[:, c * width : (c + 1) * width] = own[c][...] + far[c][...].astype(F32)
+        cols = slice(c * width, (c + 1) * width)
+        out[:, cols] = own[c][:rows, :] + far[c][:rows, :].astype(F32)
+        low = jnp.sum(far[c][rows:, :].astype(F32), axis=0, keepdims=True)
+        bias[:, cols] = own[c][rows : rows + 1, :] + low
 
 
 def on_device(sizes, *args):
@@ -334,9 +356,10 @@
     packed = table_call(
         functools.partial(pack_kernel, groups, per_device),
         1,
-        sds((groups, capacity, rows, BLK), BF),
+        [sds((capacity, rows, BLK), BF)] * groups,
         [pltpu.SMEM((groups,), jnp.int32)],
     )(*tables, cross_blocks)
+    dense_tied, _ = tie(dense, packed[0])
     moved = [packed[0]] + [swap(packed[kk], kk) for kk in range(1, groups)]
     shard = table_call(
         functools.partial(compact_kernel, groups, per_device),
@@ -360,7 +383,7 @@
         out_specs=[block(BF), block(BF), block(F32), line],
         out_shape=[narrow, narrow, wide, sds((1, local_width), F32)],
         compiler_params=params(("arbitrary",)),
-    )(dense, bottom_weight, bottom_bias.reshape(1, -1), cotangent)
+    )(dense_tied, bottom_weight, bottom_bias.reshape(1, -1), cotangent)
 
     if nx == 2:
         far = lax.ppermute(start, "x", [(0, 1), (1, 0)])
@@ -369,10 +392,29 @@
     else:
         pieces = [start] + [swap(start, kk) for kk in range(1, groups)]
 
+    plane = ny * out_rows
+    order = ring_order(nz)
+    dense_parts = []
+    for s in range(nz):
+        ahead = ring_from("z", nz, -s)
+        cut = lax.dynamic_slice_in_dim(dense, ahead * plane, plane, 1)
+        if s > 0:
+            cut = lax.ppermute(cut, "z", [(order[p], order[(p + s) % nz]) for p in range(nz)])
+        dense_parts.append(cut)
+
+    bias = bias_mixed
+    for piece in ring_gather(bias, "z", nz)[1:]:
+        bias = bias + piece
+    for piece in ring_gather(bias, "y", ny)[1:]:
+        bias = bias + piece
+
     shards = []
     for piece in ring_gather(shard, "z", nz):
+        if shards:
+            piece, shards[-1] = tie(piece, shards[-1])
         shards += ring_gather(piece, "y", ny)
 
+    low_late, _ = tie(low, shards[-1])
     tabs = [smem((width,), jnp.int32), smem((width,), jnp.int32), pltpu.SemaphoreType.DMA((width,))]
     sbuf = pltpu.VMEM((width, row_count, BLK), BF)
     block_grads = table_call(
@@ -381,13 +423,13 @@
         sds((n_dp, width, rows, BLK), BF),
         [sbuf, pltpu.VMEM((BLK, BLK), BF)] + tabs,
         in_specs=[ANY] * groups + [VMEM],
-    )(*tables, *pieces, low)
+    )(*tables, *pieces, low_late)
     summed = lax.psum_scatter(block_grads, ("z", "y"), scatter_dimension=0, tiled=True)
     summed = summed.reshape(width, rows, BLK)
     returned = table_call(
         functools.partial(expand_kernel, groups, per_device),
         1,
-        sds((groups, capacity, rows, BLK), BF),
+        [sds((capacity, rows, BLK), BF)] * groups,
     )(*tables, summed)
     returned = [returned[0]] + [swap(returned[kk], kk) for kk in range(1, groups)]
     grad_blocks = table_call(
@@ -397,6 +439,7 @@
         [pltpu.SMEM((groups,), jnp.int32)],
     )(*tables, *returned)
 
+    cotangent, *_ = tie(cotangent, bias, *dense_parts)
     cross_out, base, back_same, back_other = table_call(
         functools.partial(cross_kernel, groups, per_device, nx, nz, ny),
         groups + 4 + n_dp,
@@ -418,19 +461,9 @@
     )(*tables, *pieces, low, start, cotangent, cross_bias.reshape(per_device, 1, BLK), *shards)
     across = lax.ppermute(back_other, "core", [(0, 1), (1, 0)])
 
-    plane = ny * out_rows
-    order = ring_order(nz)
-    dense_parts = []
-    for s in range(nz):
-        ahead = ring_from("z", nz, -s)
-        cut = lax.dynamic_slice_in_dim(dense, ahead * plane, plane, 1)
-        if s > 0:
-            cut = lax.ppermute(cut, "z", [(order[p], order[(p + s) % nz]) for p in range(nz)])
-        dense_parts.append(cut)
-
     chunks = 2 if per_device % 2 == 0 else 1
     span = per_device // chunks
-    owns, fars, sums = [], [], []
+    owns, fars = [], []
     for c in range(chunks):
         sl = slice(c * span, (c + 1) * span)
         carried = None
@@ -442,27 +475,26 @@
         first = c * span
         shifted = pl.BlockSpec((1, row_count, BLK), lambda i: (i + first, 0, 0))
         plain = pl.BlockSpec((1, row_count, BLK), lambda i: (i, 0, 0))
-        grad_low, sum_c = pl.pallas_call(
+        grad_low = pl.pallas_call(
             pre_kernel,
             grid=(span,),
             in_specs=[shifted, shifted, plain, shifted],
-            out_specs=[plain, line],
-            out_shape=[sds((span, row_count, BLK), BF), sds((1, span * BLK), F32)],
+            out_specs=plain,
+            out_shape=sds((span, row_count, BLK), BF),
             compiler_params=params(("arbitrary",)),
         )(base, across[0], carried, slope)
-        sums.append(sum_c)
         gathered = ring_gather(grad_low, "z", nz)
         own, send = pl.pallas_call(
             functools.partial(weight_grad_kernel, nz, ny, out_rows),
             grid=(span,),
             in_specs=[plain] * nz + [pl.BlockSpec((row_count, plane), lambda i: (0, 0))] * nz,
             out_specs=[
-                pl.BlockSpec((out_rows, BLK), lambda i: (0, i)),
-                pl.BlockSpec((ny - 1, out_rows, BLK), lambda i: (0, 0, i)),
+                pl.BlockSpec((out_rows + EXTRA, BLK), lambda i: (0, i)),
+                pl.BlockSpec((ny - 1, out_rows + EXTRA, BLK), lambda i: (0, 0, i)),
             ],
             out_shape=[
-                sds((out_rows, span * BLK), F32),
-                sds((ny - 1, out_rows, span * BLK), BF),
+                sds((out_rows + EXTRA, span * BLK), F32),
+                sds((ny - 1, out_rows + EXTRA, span * BLK), BF),
             ],
             compiler_params=params(("arbitrary",)),
         )(*gathered, *dense_parts)
@@ -474,21 +506,15 @@
             carried = lax.ppermute(term, "y", ring_hop(ny))
         owns.append(own)
         fars.append(carried)
-    grad_bottom = pl.pallas_call(
-        functools.partial(final_kernel, chunks, span * BLK),
+    grad_bottom, bias_pre = pl.pallas_call(
+        functools.partial(final_kernel, chunks, span * BLK, out_rows),
         in_specs=[VMEM] * (2 * chunks),
-        out_specs=VMEM,
-        out_shape=sds((out_rows, local_width), F32),
+        out_specs=[VMEM, VMEM],
+        out_shape=[sds((out_rows, local_width), F32), sds((1, local_width), F32)],
         compiler_params=params(),
     )(*owns, *fars)
 
-    bias = jnp.concatenate([bias_mixed] + sums, axis=1)
-    for piece in ring_gather(bias, "z", nz)[1:]:
-        bias = bias + piece
-    for piece in ring_gather(bias, "y", ny)[1:]:
-        bias = bias + piece
-    bias = bias.reshape(2, local_width)
-    return cross_out, grad_bottom, bias[1], grad_blocks, bias[0]
+    return cross_out, grad_bottom, bias_pre.reshape(-1), grad_blocks, bias.reshape(-1)
 
 
 def solution(mesh):

time: 500 us -> 400 us (0.80)
  waiting for transfers between devices: 346 us -> 231 us
  starting transfers between devices: 48.6 us -> 63.6 us
    ppermute x17, waiting for transfers between devices: 196 us -> 147 us  [ring_gather(): pieces.append(lax.ppermute(pieces[-1], axis, ring_hop(n)))]
    ppermute x1, waiting for transfers between devices: 34.6 us -> 7.67 us  [on_device(): far = lax.ppermute(start, 'x', [(0, 1), (1, 0)])]
    ppermute x3, waiting for transfers between devices: 41.8 us -> 17 us  [on_device(): lax.ppermute(cut, 'z', [(order[p], order[(p + s) % nz]) for p in range(nz)])]
    ppermute x17, starting transfers between devices: 33.6 us -> 50.7 us  [ring_gather(): pieces.append(lax.ppermute(pieces[-1], axis, ring_hop(n)))]
    ppermute x2, waiting for transfers between devices: 23.7 us -> 17 us  [on_device(): carried = lax.ppermute(term.astype(BF), 'x', ring_hop(nx))]
  transfers between devices with their start and end apart: 35 -> 35, of which waited for: 23 -> 24; matrix products, arithmetic and copies ran while one was open for 2% -> 1% of each run, Pallas kernels for 10% -> 14%
where the time goes in v2:
time: 400 us; the launch traced here: 399 us
  waiting for transfers between devices  231 us (58%)
  Pallas kernels  75.7 us (19%)
  starting transfers between devices  63.6 us (16%)
  between operations  14.3 us (4%)
  local copies, waits for them, and re-layouts  12.1 us (3%)
    ppermute x17, waiting for transfers between devices, ring_gather(): pieces.append(lax.ppermute(pieces[-1], axis, ring_hop(n)))  147 us
    ppermute x17, starting transfers between devices, ring_gather(): pieces.append(lax.ppermute(pieces[-1], axis, ring_hop(n)))  50.7 us
    ppermute x2, waiting for transfers between devices, on_device(): carried = lax.ppermute(term, 'y', ring_hop(ny))  26.6 us
    ppermute x2, waiting for transfers between devices, on_device(): carried = lax.ppermute(term.astype(BF), 'x', ring_hop(nx))  17 us
    ppermute x3, waiting for transfers between devices, on_device(): lax.ppermute(cut, 'z', [(order[p], order[(p + s) % nz]) for p in range(nz)])  17 us
    pallas_call x1, Pallas kernels, on_device(): table_call(functools.partial(cross_kernel, groups, per_device, nx, nz, ny...  14.7 us
    pallas_call x1, Pallas kernels, on_device(): pl.pallas_call(bottom_kernel, grid=(per_device,), in_specs=[pl.BlockSpec(...  13.2 us
    pallas_call x2, Pallas kernels, on_device(): pl.pallas_call(functools.partial(weight_grad_kernel, nz, ny, out_rows), g...  12.9 us
  transfers between devices with their start and end apart: 35, of which 24 were waited for; matrix products, arithmetic and copies ran while one was open for 1% of the time, Pallas kernels for 14%

profile of v2, /device:TPU:0, one launch (start us, length us, event | category | flops | bytes accessed | tf_op | source)
XLA Modules:
  0.0 398.9 jit_solution(811676307975025687)
XLA Ops:
  7.2 3.0 shard_map.128
  10.7 2.4 collective-permute-start.11
  13.3 5.8 %collective-permute-done.11.refs_2_ = bf16[3,64,512]{2,1,0:T(8,128)(2,1)S(1)} collective-permute-done((bf16[3,64,512]{2,1,0:T(8,128)(2,1)}, bf16[3,64,512]{2,1,0:T(8,128)(2,1)S(1)}, u32[]{:S(2)}, u32[]{:S(2)}) %collective-permute-start.11) | collective-permute-done | bytes 196640 | tf_op jit(solution)/shard_map/ppermute | solution.py:354
  19.1 3.8 collective-permute-done.12.refs_3_
  23.6 3.3 shard_map.130.refs_8_
  26.9 1.6 collective-permute-start.14
  28.5 2.6 collective-permute-start.13
  31.0 13.2 %shard_map.129 = (bf16[8,192,512]{2,1,0:T(8,128)(2,1)}, bf16[8,192,512]{2,1,0:T(8,128)(2,1)}, f32[8,192,512]{2,1,0:T(8,128)}, f32[1,4096]{1,0:T(1,128)}) custom-call(bf16[192,2048]{1,0:T(8,128)(2,1)} %dense, bf16[2048,4096]{1,0:T(8,128)(2,1)} %weight.1, f32[1,4096]{1,0:T(1,128)} %bitcast.16, bf16[192,4096]{1,0:T(8,128)(2,1)} %refs_6_), custom_call_target="tpu_custom_call" | custom-call | tf_op jit(solution)/shard_map/pallas_call | solution.py:374
  44.2 1.5 collective-permute-start.1
  46.7 1.6 collective-permute-done.13.refs_10_
  48.8 3.3 collective-permute-start.15
  52.0 14.7 %collective-permute-done.16.refs_11_ = bf16[12,64,512]{2,1,0:T(8,128)(2,1)S(1)} collective-permute-done((bf16[12,64,512]{2,1,0:T(8,128)(2,1)S(1)}, bf16[12,64,512]{2,1,0:T(8,128)(2,1)S(1)}, u32[]{:S(2)}, u32[]{:S(2)}) %collective-permute-start.16) | collective-permute-done | bytes 786464 | tf_op jit(solution)/shard_map/ppermute | solution.py:57
  67.8 1.5 collective-permute-start.18
  69.3 3.4 collective-permute-start.17
  72.7 7.7 %collective-permute-done.1.refs_2_ = bf16[8,192,512]{2,1,0:T(8,128)(2,1)S(1)} collective-permute-done((bf16[8,192,512]{2,1,0:T(8,128)(2,1)}, bf16[8,192,512]{2,1,0:T(8,128)(2,1)S(1)}, u32[]{:S(2)}, u32[]{:S(2)}) %collective-permute-start.1) | collective-permute-done | bytes 1572896 | tf_op jit(solution)/shard_map/ppermute | solution.py:389
  80.4 4.8 %collective-permute-done.18.refs_13_ = bf16[12,64,512]{2,1,0:T(8,128)(2,1)S(1)} collective-permute-done((bf16[12,64,512]{2,1,0:T(8,128)(2,1)S(1)}, bf16[12,64,512]{2,1,0:T(8,128)(2,1)S(1)}, u32[]{:S(2)}, u32[]{:S(2)}) %collective-permute-start.18) | collective-permute-done | bytes 786464 | tf_op jit(solution)/shard_map/ppermute | solution.py:57
  85.2 2.1 collective-permute-done.17.refs_14_
  87.7 15.7 %collective-permute-done.19.refs_15_ = bf16[12,64,512]{2,1,0:T(8,128)(2,1)S(1)} collective-permute-done((bf16[12,64,512]{2,1,0:T(8,128)(2,1)S(1)}, bf16[12,64,512]{2,1,0:T(8,128)(2,1)S(1)}, u32[]{:S(2)}, u32[]{:S(2)}) %collective-permute-start.19) | collective-permute-done | bytes 786464 | tf_op jit(solution)/shard_map/ppermute | solution.py:57
  106.7 8.5 %shard_map.137 = bf16[8,12,64,512]{3,2,1,0:T(8,128)(2,1)} custom-call(s32[4,10]{1,0:T(4,128)} %inb.11, s32[4,10]{1,0:T(4,128)} %outb.11, s32[4]{0:T(128)} %live.11, bf16[8,192,512]{2,1,0:T(8,128)(2,1)} %get-tuple-element.38.refs_0_.refs_5_, bf16[8,192,512]{2,1,0:T(8,128)(2,1)} %copy-done.1, bf16[8,192,512]{2,1,0:T(8,128)(2,1)} %copy-done, ...), custom_call_target="tpu_custom_call" | custom-call | tf_op jit(solution)/shard_map/pallas_call | solution.py:420
  115.9 3.3 collective-permute-start.3
  120.6 3.2 collective-permute-start.4
  123.8 1.9 collective-permute-done.4
  125.7 3.2 collective-permute-start.5
  129.6 2.9 collective-permute-start.7
  134.4 3.2 collective-permute-done.6
  138.2 17.0 %collective-permute-done.9.refs_7_ = bf16[192,512]{1,0:T(8,128)(2,1)S(1)} collective-permute-done((bf16[192,512]{1,0:T(8,128)(2,1)S(1)}, bf16[192,512]{1,0:T(8,128)(2,1)S(1)}, u32[]{:S(2)}, u32[]{:S(2)}) %collective-permute-start.9) | collective-permute-done | bytes 196640 | tf_op jit(solution)/shard_map/ppermute | solution.py:402
  155.3 14.7 %shard_map.131 = (bf16[192,4096]{1,0:T(8,128)(2,1)}, f32[8,192,512]{2,1,0:T(8,128)}, bf16[1,8,192,512]{3,2,1,0:T(8,128)(2,1)}, bf16[2,8,192,512]{3,2,1,0:T(8,128)(2,1)}) custom-call(s32[4,10]{1,0:T(4,128)} %inb.11, s32[4,10]{1,0:T(4,128)} %outb.11, s32[4]{0:T(128)} %live.11, bf16[8,192,512]{2,1,0:T(8,128)(2,1)} %get-tuple-element.38.refs_0_.refs_5_, ...), custom_call_target="tpu_custom_call" | custom-call | tf_op jit(solution)/shard_map/pallas_call | solution.py:443
  170.1 5.9 %collective-permute-done.20 = bf16[2,8,192,512]{3,2,1,0:T(8,128)(2,1)S(1)} collective-permute-done((bf16[2,8,192,512]{3,2,1,0:T(8,128)(2,1)}, bf16[2,8,192,512]{3,2,1,0:T(8,128)(2,1)S(1)}, u32[]{:S(2)}, u32[]{:S(2)}) %collective-permute-start.20) | collective-permute-done | bytes 3145760 | tf_op jit(solution)/shard_map/ppermute | solution.py:462
  175.9 1.8 fusion.1
  177.9 2.0 collective-permute-start.25
  181.2 17.0 %collective-permute-done.21.far = bf16[4,192,512]{2,1,0:T(8,128)(2,1)S(1)} collective-permute-done((bf16[4,192,512]{2,1,0:T(8,128)(2,1)S(1)}, bf16[4,192,512]{2,1,0:T(8,128)(2,1)S(1)}, u32[]{:S(2)}, u32[]{:S(2)}) %collective-permute-start.21) | collective-permute-done | bytes 786464 | tf_op jit(solution)/shard_map/ppermute | solution.py:474
  199.1 4.1 %shard_map.132.refs_0_ = bf16[4,192,512]{2,1,0:T(8,128)(2,1)} custom-call(f32[8,192,512]{2,1,0:T(8,128)} %get-tuple-element.52.base, bf16[8,192,512]{2,1,0:T(8,128)(2,1)} %slice_bitcast_fusion.here, bf16[4,192,512]{2,1,0:T(8,128)(2,1)} %copy-done.14, f32[8,192,512]{2,1,0:T(8,128)} %get-tuple-element.55.slope), custom_call_target="tpu_custom_call" | custom-call | tf_op jit(solution)/shard_map/pallas_call | solution.py:478
  203.3 11.5 %collective-permute-start.22 = (bf16[4,192,512]{2,1,0:T(8,128)(2,1)}, bf16[4,192,512]{2,1,0:T(8,128)(2,1)S(1)}, u32[]{:S(2)}, u32[]{:S(2)}) collective-permute-start(bf16[4,192,512]{2,1,0:T(8,128)(2,1)} %shard_map.132.refs_0_), channel_id=1, source_target_pairs={{0,16},{16,24},{24,8},{8,0},{1,17},{17,25},{25,9},{9,1},{2,18},{18... | collective-permute-start | bytes 2359304 | tf_op jit(solution)/shard_map/ppermute | solution.py:57
  215.7 4.1 %shard_map.134.refs_0_ = bf16[4,192,512]{2,1,0:T(8,128)(2,1)} custom-call(f32[8,192,512]{2,1,0:T(8,128)} %get-tuple-element.52.base, bf16[8,192,512]{2,1,0:T(8,128)(2,1)} %slice_bitcast_fusion.here, bf16[4,192,512]{2,1,0:T(8,128)(2,1)} %copy-done.13, f32[8,192,512]{2,1,0:T(8,128)} %get-tuple-element.55.slope), custom_call_target="tpu_custom_call" | custom-call | tf_op jit(solution)/shard_map/pallas_call | solution.py:478
  219.8 11.1 %collective-permute-start.26 = (bf16[4,192,512]{2,1,0:T(8,128)(2,1)}, bf16[4,192,512]{2,1,0:T(8,128)(2,1)S(1)}, u32[]{:S(2)}, u32[]{:S(2)}) collective-permute-start(bf16[4,192,512]{2,1,0:T(8,128)(2,1)} %shard_map.134.refs_0_), channel_id=1, source_target_pairs={{0,16},{16,24},{24,8},{8,0},{1,17},{17,25},{25,9},{9,1},{2,18},{18... | collective-permute-start | bytes 2359304 | tf_op jit(solution)/shard_map/ppermute | solution.py:57
  230.8 19.7 %collective-permute-done.22.refs_1_ = bf16[4,192,512]{2,1,0:T(8,128)(2,1)S(1)} collective-permute-done((bf16[4,192,512]{2,1,0:T(8,128)(2,1)}, bf16[4,192,512]{2,1,0:T(8,128)(2,1)S(1)}, u32[]{:S(2)}, u32[]{:S(2)}) %collective-permute-start.22) | collective-permute-done | bytes 786464 | tf_op jit(solution)/shard_map/ppermute | solution.py:57
  250.5 26.6 %collective-permute-done.26.refs_1_ = bf16[4,192,512]{2,1,0:T(8,128)(2,1)S(1)} collective-permute-done((bf16[4,192,512]{2,1,0:T(8,128)(2,1)}, bf16[4,192,512]{2,1,0:T(8,128)(2,1)S(1)}, u32[]{:S(2)}, u32[]{:S(2)}) %collective-permute-start.26) | collective-permute-done | bytes 786464 | tf_op jit(solution)/shard_map/ppermute | solution.py:57
  278.6 15.4 %collective-permute-done.23.refs_2_ = bf16[4,192,512]{2,1,0:T(8,128)(2,1)S(1)} collective-permute-done((bf16[4,192,512]{2,1,0:T(8,128)(2,1)S(1)}, bf16[4,192,512]{2,1,0:T(8,128)(2,1)S(1)}, u32[]{:S(2)}, u32[]{:S(2)}) %collective-permute-start.23) | collective-permute-done | bytes 786464 | tf_op jit(solution)/shard_map/ppermute | solution.py:57
  295.4 15.4 %collective-permute-done.27.refs_2_ = bf16[4,192,512]{2,1,0:T(8,128)(2,1)S(1)} collective-permute-done((bf16[4,192,512]{2,1,0:T(8,128)(2,1)S(1)}, bf16[4,192,512]{2,1,0:T(8,128)(2,1)S(1)}, u32[]{:S(2)}, u32[]{:S(2)}) %collective-permute-start.27) | collective-permute-done | bytes 786464 | tf_op jit(solution)/shard_map/ppermute | solution.py:57
  312.3 15.4 %collective-permute-done.24.refs_3_ = bf16[4,192,512]{2,1,0:T(8,128)(2,1)S(1)} collective-permute-done((bf16[4,192,512]{2,1,0:T(8,128)(2,1)S(1)}, bf16[4,192,512]{2,1,0:T(8,128)(2,1)S(1)}, u32[]{:S(2)}, u32[]{:S(2)}) %collective-permute-start.24) | collective-permute-done | bytes 786464 | tf_op jit(solution)/shard_map/ppermute | solution.py:57
  328.5 6.5 %shard_map.133 = (f32[272,2048]{1,0:T(8,128)}, bf16[1,272,2048]{2,1,0:T(8,128)(2,1)}) custom-call(bf16[4,192,512]{2,1,0:T(8,128)(2,1)} %shard_map.132.refs_0_, bf16[4,192,512]{2,1,0:T(8,128)(2,1)} %copy-done.16, bf16[4,192,512]{2,1,0:T(8,128)(2,1)} %copy-done.18, bf16[4,192,512]{2,1,0:T(8,128)(2,1)} %copy-done.20, ...), custom_call_target="tpu_custom_call" | custom-call | tf_op jit(solution)/shard_map/pallas_call | solution.py:487
  335.1 7.3 %collective-permute-done.28.refs_3_ = bf16[4,192,512]{2,1,0:T(8,128)(2,1)S(1)} collective-permute-done((bf16[4,192,512]{2,1,0:T(8,128)(2,1)S(1)}, bf16[4,192,512]{2,1,0:T(8,128)(2,1)S(1)}, u32[]{:S(2)}, u32[]{:S(2)}) %collective-permute-start.28) | collective-permute-done | bytes 786464 | tf_op jit(solution)/shard_map/ppermute | solution.py:57
  343.2 6.4 %shard_map.135 = (f32[272,2048]{1,0:T(8,128)}, bf16[1,272,2048]{2,1,0:T(8,128)(2,1)}) custom-call(bf16[4,192,512]{2,1,0:T(8,128)(2,1)} %shard_map.134.refs_0_, bf16[4,192,512]{2,1,0:T(8,128)(2,1)} %copy-done.15, bf16[4,192,512]{2,1,0:T(8,128)(2,1)} %copy-done.17, bf16[4,192,512]{2,1,0:T(8,128)(2,1)} %copy-done.19, ...), custom_call_target="tpu_custom_call" | custom-call | tf_op jit(solution)/shard_map/pallas_call | solution.py:487
  349.7 3.2 shard_map.138
  354.8 7.9 %collective-permute-done.29.refs_2_ = bf16[272,2048]{1,0:T(8,128)(2,1)S(1)} collective-permute-done((bf16[272,2048]{1,0:T(8,128)(2,1)}, bf16[272,2048]{1,0:T(8,128)(2,1)S(1)}, u32[]{:S(2)}, u32[]{:S(2)}) %collective-permute-start.29) | collective-permute-done | bytes 1114144 | tf_op jit(solution)/shard_map/ppermute | solution.py:506
  362.8 18.7 %collective-permute-done.30.refs_3_ = bf16[272,2048]{1,0:T(8,128)(2,1)S(1)} collective-permute-done((bf16[272,2048]{1,0:T(8,128)(2,1)}, bf16[272,2048]{1,0:T(8,128)(2,1)S(1)}, u32[]{:S(2)}, u32[]{:S(2)}) %collective-permute-start.30) | collective-permute-done | bytes 1114144 | tf_op jit(solution)/shard_map/ppermute | solution.py:506
  382.5 5.3 %shard_map.136 = (f32[256,4096]{1,0:T(8,128)}, f32[1,4096]{1,0:T(1,128)}) custom-call(f32[272,2048]{1,0:T(8,128)} %get-tuple-element.56.refs_0_, f32[272,2048]{1,0:T(8,128)} %get-tuple-element.57.refs_1_, bf16[272,2048]{1,0:T(8,128)(2,1)} %copy-done.4, bf16[272,2048]{1,0:T(8,128)(2,1)} %copy-done.5), custom_call_target="tpu_custom_call" | custom-call | tf_op jit(solution)/shard_map/pallas_call | solution.py:509
  388.6 3.4 shard_map.139
  (102 shorter events, 26.3 us)
Async XLA Ops:
  7.2 342.5 %reduce-scatter.2.cloned.1.call-start = ((), (), s32[]{:S(2)}) async-start(), calls=%async_computation.1 | async-start | bytes 7077888 | tf_op jit(solution)/shard_map/reduce_scatter | solution.py:427
  10.2 3.1 collective-permute-start.10
  10.7 8.4 %collective-permute-start.11 = (bf16[3,64,512]{2,1,0:T(8,128)(2,1)}, bf16[3,64,512]{2,1,0:T(8,128)(2,1)S(1)}, u32[]{:S(2)}, u32[]{:S(2)}) collective-permute-start(bf16[3,64,512]{2,1,0:T(8,128)(2,1)} %get-tuple-element.43), channel_id=1, source_target_pairs={{0,2},{1,3},{2,0},{3,1},{4,6},{5,7},{6,4},{7,5},{8,10},{9,11},{10,... | collective-permute-start | bytes 589832 | tf_op jit(solution)/shard_map/ppermute | solution.py:354
  13.1 9.8 %collective-permute-start.12 = (bf16[3,64,512]{2,1,0:T(8,128)(2,1)}, bf16[3,64,512]{2,1,0:T(8,128)(2,1)S(1)}, u32[]{:S(2)}, u32[]{:S(2)}) collective-permute-start(bf16[3,64,512]{2,1,0:T(8,128)(2,1)} %get-tuple-element.44), channel_id=1, source_target_pairs={{0,3},{1,2},{2,1},{3,0},{4,7},{5,6},{6,5},{7,4},{8,11},{9,10},{10,... | collective-permute-start | bytes 589832 | tf_op jit(solution)/shard_map/ppermute | solution.py:354
  26.9 19.8 %collective-permute-start.14 = (bf16[12,64,512]{2,1,0:T(8,128)(2,1)}, bf16[12,64,512]{2,1,0:T(8,128)(2,1)S(1)}, u32[]{:S(2)}, u32[]{:S(2)}) collective-permute-start(bf16[12,64,512]{2,1,0:T(8,128)(2,1)} %shard_map.130.refs_8_), channel_id=1, source_target_pairs={{0,4},{4,0},{1,5},{5,1},{2,6},{6,2},{3,7},{7,3},{8,12},{12,8},{9,1... | collective-permute-start | bytes 2359304 | tf_op jit(solution)/shard_map/ppermute | solution.py:57
  28.5 19.8 %collective-permute-start.13 = (bf16[12,64,512]{2,1,0:T(8,128)(2,1)}, bf16[12,64,512]{2,1,0:T(8,128)(2,1)S(1)}, u32[]{:S(2)}, u32[]{:S(2)}) collective-permute-start(bf16[12,64,512]{2,1,0:T(8,128)(2,1)} %shard_map.130.refs_8_), channel_id=1, source_target_pairs={{0,16},{16,24},{24,8},{8,0},{1,17},{17,25},{25,9},{9,1},{2,18},{18... | collective-permute-start | bytes 2359304 | tf_op jit(solution)/shard_map/ppermute | solution.py:57
  44.2 36.2 %collective-permute-start.1 = (bf16[8,192,512]{2,1,0:T(8,128)(2,1)}, bf16[8,192,512]{2,1,0:T(8,128)(2,1)S(1)}, u32[]{:S(2)}, u32[]{:S(2)}) collective-permute-start(bf16[8,192,512]{2,1,0:T(8,128)(2,1)} %get-tuple-element.38.refs_0_.refs_5_), channel_id=1, source_target_pairs={{0,2},{2,0},{1,3},{3,1},{4,6},{6,4},{5,7},{7,5},{8,10},{10,8},{9,1... | collective-permute-start | bytes 4718600 | tf_op jit(solution)/shard_map/ppermute | solution.py:389
  46.7 68.4 %copy-start.6 = (bf16[12,64,512]{2,1,0:T(8,128)(2,1)}, bf16[12,64,512]{2,1,0:T(8,128)(2,1)S(1)}, u32[]{:S(2)}) copy-start(bf16[12,64,512]{2,1,0:T(8,128)(2,1)S(1)} %collective-permute-done.14.refs_9_) | copy-start | bytes 2359300
  48.3 66.9 %copy-start.7 = (bf16[12,64,512]{2,1,0:T(8,128)(2,1)}, bf16[12,64,512]{2,1,0:T(8,128)(2,1)S(1)}, u32[]{:S(2)}) copy-start(bf16[12,64,512]{2,1,0:T(8,128)(2,1)S(1)} %collective-permute-done.13.refs_10_) | copy-start | bytes 2359300
  48.3 18.5 %collective-permute-start.16 = (bf16[12,64,512]{2,1,0:T(8,128)(2,1)S(1)}, bf16[12,64,512]{2,1,0:T(8,128)(2,1)S(1)}, u32[]{:S(2)}, u32[]{:S(2)}) collective-permute-start(bf16[12,64,512]{2,1,0:T(8,128)(2,1)S(1)} %collective-permute-done.13.refs_10_), channel_id=1, source_target_pairs={{0,4},{4,0},{1,5},{5,1},{2,6},{6,2},{3,7},{7,3},{8,12},{12,8},{9,1... | collective-permute-start | bytes 2359304 | tf_op jit(solution)/shard_map/ppermute | solution.py:57
  48.8 19.0 %collective-permute-start.15 = (bf16[12,64,512]{2,1,0:T(8,128)(2,1)S(1)}, bf16[12,64,512]{2,1,0:T(8,128)(2,1)S(1)}, u32[]{:S(2)}, u32[]{:S(2)}) collective-permute-start(bf16[12,64,512]{2,1,0:T(8,128)(2,1)S(1)} %collective-permute-done.13.refs_10_), channel_id=1, source_target_pairs={{0,16},{16,24},{24,8},{8,0},{1,17},{17,25},{25,9},{9,1},{2,18},{18... | collective-permute-start | bytes 2359304 | tf_op jit(solution)/shard_map/ppermute | solution.py:57
  66.8 48.4 %copy-start.8 = (bf16[12,64,512]{2,1,0:T(8,128)(2,1)}, bf16[12,64,512]{2,1,0:T(8,128)(2,1)S(1)}, u32[]{:S(2)}) copy-start(bf16[12,64,512]{2,1,0:T(8,128)(2,1)S(1)} %collective-permute-done.16.refs_11_) | copy-start | bytes 2359300
  67.8 36.6 %copy-start.9 = (bf16[12,64,512]{2,1,0:T(8,128)(2,1)}, bf16[12,64,512]{2,1,0:T(8,128)(2,1)S(1)}, u32[]{:S(2)}) copy-start(bf16[12,64,512]{2,1,0:T(8,128)(2,1)S(1)} %collective-permute-done.15.refs_12_) | copy-start | bytes 2359300
  67.8 17.4 %collective-permute-start.18 = (bf16[12,64,512]{2,1,0:T(8,128)(2,1)S(1)}, bf16[12,64,512]{2,1,0:T(8,128)(2,1)S(1)}, u32[]{:S(2)}, u32[]{:S(2)}) collective-permute-start(bf16[12,64,512]{2,1,0:T(8,128)(2,1)S(1)} %collective-permute-done.15.refs_12_), channel_id=1, source_target_pairs={{0,4},{4,0},{1,5},{5,1},{2,6},{6,2},{3,7},{7,3},{8,12},{12,8},{9,1... | collective-permute-start | bytes 2359304 | tf_op jit(solution)/shard_map/ppermute | solution.py:57
  69.3 17.9 %collective-permute-start.17 = (bf16[12,64,512]{2,1,0:T(8,128)(2,1)S(1)}, bf16[12,64,512]{2,1,0:T(8,128)(2,1)S(1)}, u32[]{:S(2)}, u32[]{:S(2)}) collective-permute-start(bf16[12,64,512]{2,1,0:T(8,128)(2,1)S(1)} %collective-permute-done.15.refs_12_), channel_id=1, source_target_pairs={{0,16},{16,24},{24,8},{8,0},{1,17},{17,25},{25,9},{9,1},{2,18},{18... | collective-permute-start | bytes 2359304 | tf_op jit(solution)/shard_map/ppermute | solution.py:57
  72.7 30.8 %collective-permute-start = (bf16[8,192,512]{2,1,0:T(8,128)(2,1)}, bf16[8,192,512]{2,1,0:T(8,128)(2,1)S(1)}, u32[]{:S(2)}, u32[]{:S(2)}) collective-permute-start(bf16[8,192,512]{2,1,0:T(8,128)(2,1)} %get-tuple-element.38.refs_0_.refs_5_), channel_id=1, source_target_pairs={{0,1},{1,0},{2,3},{3,2},{4,5},{5,4},{6,7},{7,6},{8,9},{9,8},{10,11... | collective-permute-start | bytes 4718600 | tf_op jit(solution)/shard_map/ppermute | solution.py:391
  80.4 24.0 %copy-start = (bf16[8,192,512]{2,1,0:T(8,128)(2,1)}, bf16[8,192,512]{2,1,0:T(8,128)(2,1)S(1)}, u32[]{:S(2)}) copy-start(bf16[8,192,512]{2,1,0:T(8,128)(2,1)S(1)} %collective-permute-done.1.refs_2_) | copy-start | bytes 4718596
  80.4 24.0 %collective-permute-start.2 = (bf16[8,192,512]{2,1,0:T(8,128)(2,1)S(1)}, bf16[8,192,512]{2,1,0:T(8,128)(2,1)S(1)}, u32[]{:S(2)}, u32[]{:S(2)}) collective-permute-start(bf16[8,192,512]{2,1,0:T(8,128)(2,1)S(1)} %collective-permute-done.1.refs_2_), channel_id=1, source_target_pairs={{0,1},{1,0},{2,3},{3,2},{4,5},{5,4},{6,7},{7,6},{8,9},{9,8},{10,11... | collective-permute-start | bytes 4718600 | tf_op jit(solution)/shard_map/ppermute | solution.py:391
  85.2 18.3 %copy-start.10 = (bf16[12,64,512]{2,1,0:T(8,128)(2,1)}, bf16[12,64,512]{2,1,0:T(8,128)(2,1)S(1)}, u32[]{:S(2)}) copy-start(bf16[12,64,512]{2,1,0:T(8,128)(2,1)S(1)} %collective-permute-done.18.refs_13_) | copy-start | bytes 2359300
  87.2 16.2 %copy-start.11 = (bf16[12,64,512]{2,1,0:T(8,128)(2,1)}, bf16[12,64,512]{2,1,0:T(8,128)(2,1)S(1)}, u32[]{:S(2)}) copy-start(bf16[12,64,512]{2,1,0:T(8,128)(2,1)S(1)} %collective-permute-done.17.refs_14_) | copy-start | bytes 2359300
  87.2 16.2 %collective-permute-start.19 = (bf16[12,64,512]{2,1,0:T(8,128)(2,1)S(1)}, bf16[12,64,512]{2,1,0:T(8,128)(2,1)S(1)}, u32[]{:S(2)}, u32[]{:S(2)}) collective-permute-start(bf16[12,64,512]{2,1,0:T(8,128)(2,1)S(1)} %collective-permute-done.17.refs_14_), channel_id=1, source_target_pairs={{0,4},{4,0},{1,5},{5,1},{2,6},{6,2},{3,7},{7,3},{8,12},{12,8},{9,1... | collective-permute-start | bytes 2359304 | tf_op jit(solution)/shard_map/ppermute | solution.py:57
  115.9 4.7 %collective-permute-start.3 = (f32[1,4096]{1,0:T(1,128)S(1)}, f32[1,4096]{1,0:T(1,128)S(1)}, u32[]{:S(2)}, u32[]{:S(2)}) collective-permute-start(f32[1,4096]{1,0:T(1,128)S(1)} %copy-done.30), channel_id=1, source_target_pairs={{0,16},{16,24},{24,8},{8,0},{1,17},{17,25},{25,9},{9,1},{2,18},{18... | collective-permute-start | bytes 49160 | tf_op jit(solution)/shard_map/ppermute | solution.py:57
  120.6 5.1 %collective-permute-start.4 = (f32[1,4096]{1,0:T(1,128)S(1)}, f32[1,4096]{1,0:T(1,128)S(1)}, u32[]{:S(2)}, u32[]{:S(2)}) collective-permute-start(f32[1,4096]{1,0:T(1,128)S(1)} %collective-permute-done.3), channel_id=1, source_target_pairs={{0,16},{16,24},{24,8},{8,0},{1,17},{17,25},{25,9},{9,1},{2,18},{18... | collective-permute-start | bytes 49160 | tf_op jit(solution)/shard_map/ppermute | solution.py:57
  125.7 8.0 %collective-permute-start.5 = (f32[1,4096]{1,0:T(1,128)S(1)}, f32[1,4096]{1,0:T(1,128)S(1)}, u32[]{:S(2)}, u32[]{:S(2)}) collective-permute-start(f32[1,4096]{1,0:T(1,128)S(1)} %collective-permute-done.4), channel_id=1, source_target_pairs={{0,16},{16,24},{24,8},{8,0},{1,17},{17,25},{25,9},{9,1},{2,18},{18... | collective-permute-start | bytes 49160 | tf_op jit(solution)/shard_map/ppermute | solution.py:57
  129.6 25.6 %collective-permute-start.9 = (bf16[192,512]{1,0:T(8,128)(2,1)S(1)}, bf16[192,512]{1,0:T(8,128)(2,1)S(1)}, u32[]{:S(2)}, u32[]{:S(2)}) collective-permute-start(bf16[192,512]{1,0:T(8,128)(2,1)S(1)} %get-tuple-element.69), channel_id=1, source_target_pairs={{0,8},{16,0},{24,16},{8,24},{1,9},{17,1},{25,17},{9,25},{2,10},{18... | collective-permute-start | bytes 589832 | tf_op jit(solution)/shard_map/ppermute | solution.py:402
  129.6 25.6 %collective-permute-start.7 = (bf16[192,512]{1,0:T(8,128)(2,1)S(1)}, bf16[192,512]{1,0:T(8,128)(2,1)S(1)}, u32[]{:S(2)}, u32[]{:S(2)}) collective-permute-start(bf16[192,512]{1,0:T(8,128)(2,1)S(1)} %get-tuple-element.70), channel_id=1, source_target_pairs={{0,16},{16,24},{24,8},{8,0},{1,17},{17,25},{25,9},{9,1},{2,18},{18... | collective-permute-start | bytes 589832 | tf_op jit(solution)/shard_map/ppermute | solution.py:402
  132.6 22.7 %collective-permute-start.8 = (bf16[192,512]{1,0:T(8,128)(2,1)S(1)}, bf16[192,512]{1,0:T(8,128)(2,1)S(1)}, u32[]{:S(2)}, u32[]{:S(2)}) collective-permute-start(bf16[192,512]{1,0:T(8,128)(2,1)S(1)} %get-tuple-element.72), channel_id=1, source_target_pairs={{0,24},{16,8},{24,0},{8,16},{1,25},{17,9},{25,1},{9,17},{2,26},{18... | collective-permute-start | bytes 589832 | tf_op jit(solution)/shard_map/ppermute | solution.py:402
  133.8 3.8 collective-permute-start.6
  155.2 14.8 %copy-start.23 = (bf16[192,512]{1,0:T(8,128)(2,1)}, bf16[192,512]{1,0:T(8,128)(2,1)S(1)}, u32[]{:S(2)}) copy-start(bf16[192,512]{1,0:T(8,128)(2,1)S(1)} %collective-permute-done.8.refs_6_) | copy-start | bytes 589828
  170.0 5.9 %collective-permute-start.20 = (bf16[2,8,192,512]{3,2,1,0:T(8,128)(2,1)}, bf16[2,8,192,512]{3,2,1,0:T(8,128)(2,1)S(1)}, u32[]{:S(2)}, u32[]{:S(2)}) collective-permute-start(bf16[2,8,192,512]{3,2,1,0:T(8,128)(2,1)} %get-tuple-element.53), channel_id=1, source_target_pairs={{0,1},{1,0},{2,3},{3,2},{4,5},{5,4},{6,7},{7,6},{8,9},{9,8},{10,11... | collective-permute-start | bytes 9437192 | tf_op jit(solution)/shard_map/ppermute | solution.py:462
  177.8 20.5 %collective-permute-start.21 = (bf16[4,192,512]{2,1,0:T(8,128)(2,1)S(1)}, bf16[4,192,512]{2,1,0:T(8,128)(2,1)S(1)}, u32[]{:S(2)}, u32[]{:S(2)}) collective-permute-start(bf16[4,192,512]{2,1,0:T(8,128)(2,1)S(1)} %get-tuple-element.68), channel_id=1, source_target_pairs={{0,2},{2,0},{1,3},{3,1},{4,6},{6,4},{5,7},{7,5},{8,10},{10,8},{9,1... | collective-permute-start | bytes 2359304 | tf_op jit(solution)/shard_map/ppermute | solution.py:474
  177.9 36.9 %collective-permute-start.25 = (bf16[4,192,512]{2,1,0:T(8,128)(2,1)S(1)}, bf16[4,192,512]{2,1,0:T(8,128)(2,1)S(1)}, u32[]{:S(2)}, u32[]{:S(2)}) collective-permute-start(bf16[4,192,512]{2,1,0:T(8,128)(2,1)S(1)} %get-tuple-element.67), channel_id=1, source_target_pairs={{0,2},{2,0},{1,3},{3,1},{4,6},{6,4},{5,7},{7,5},{8,10},{10,8},{9,1... | collective-permute-start | bytes 2359304 | tf_op jit(solution)/shard_map/ppermute | solution.py:474
  203.3 47.2 %collective-permute-start.22 = (bf16[4,192,512]{2,1,0:T(8,128)(2,1)}, bf16[4,192,512]{2,1,0:T(8,128)(2,1)S(1)}, u32[]{:S(2)}, u32[]{:S(2)}) collective-permute-start(bf16[4,192,512]{2,1,0:T(8,128)(2,1)} %shard_map.132.refs_0_), channel_id=1, source_target_pairs={{0,16},{16,24},{24,8},{8,0},{1,17},{17,25},{25,9},{9,1},{2,18},{18... | collective-permute-start | bytes 2359304 | tf_op jit(solution)/shard_map/ppermute | solution.py:57
  219.8 57.3 %collective-permute-start.26 = (bf16[4,192,512]{2,1,0:T(8,128)(2,1)}, bf16[4,192,512]{2,1,0:T(8,128)(2,1)S(1)}, u32[]{:S(2)}, u32[]{:S(2)}) collective-permute-start(bf16[4,192,512]{2,1,0:T(8,128)(2,1)} %shard_map.134.refs_0_), channel_id=1, source_target_pairs={{0,16},{16,24},{24,8},{8,0},{1,17},{17,25},{25,9},{9,1},{2,18},{18... | collective-permute-start | bytes 2359304 | tf_op jit(solution)/shard_map/ppermute | solution.py:57
  250.5 77.1 %copy-start.16 = (bf16[4,192,512]{2,1,0:T(8,128)(2,1)}, bf16[4,192,512]{2,1,0:T(8,128)(2,1)S(1)}, u32[]{:S(2)}) copy-start(bf16[4,192,512]{2,1,0:T(8,128)(2,1)S(1)} %collective-permute-done.22.refs_1_) | copy-start | bytes 2359300
  250.5 43.4 %collective-permute-start.23 = (bf16[4,192,512]{2,1,0:T(8,128)(2,1)S(1)}, bf16[4,192,512]{2,1,0:T(8,128)(2,1)S(1)}, u32[]{:S(2)}, u32[]{:S(2)}) collective-permute-start(bf16[4,192,512]{2,1,0:T(8,128)(2,1)S(1)} %collective-permute-done.22.refs_1_), channel_id=1, source_target_pairs={{0,16},{16,24},{24,8},{8,0},{1,17},{17,25},{25,9},{9,1},{2,18},{18... | collective-permute-start | bytes 2359304 | tf_op jit(solution)/shard_map/ppermute | solution.py:57
  277.1 57.9 %copy-start.15 = (bf16[4,192,512]{2,1,0:T(8,128)(2,1)}, bf16[4,192,512]{2,1,0:T(8,128)(2,1)S(1)}, u32[]{:S(2)}) copy-start(bf16[4,192,512]{2,1,0:T(8,128)(2,1)S(1)} %collective-permute-done.26.refs_1_) | copy-start | bytes 2359300
  277.1 33.7 %collective-permute-start.27 = (bf16[4,192,512]{2,1,0:T(8,128)(2,1)S(1)}, bf16[4,192,512]{2,1,0:T(8,128)(2,1)S(1)}, u32[]{:S(2)}, u32[]{:S(2)}) collective-permute-start(bf16[4,192,512]{2,1,0:T(8,128)(2,1)S(1)} %collective-permute-done.26.refs_1_), channel_id=1, source_target_pairs={{0,16},{16,24},{24,8},{8,0},{1,17},{17,25},{25,9},{9,1},{2,18},{18... | collective-permute-start | bytes 2359304 | tf_op jit(solution)/shard_map/ppermute | solution.py:57
  293.9 33.7 %copy-start.18 = (bf16[4,192,512]{2,1,0:T(8,128)(2,1)}, bf16[4,192,512]{2,1,0:T(8,128)(2,1)S(1)}, u32[]{:S(2)}) copy-start(bf16[4,192,512]{2,1,0:T(8,128)(2,1)S(1)} %collective-permute-done.23.refs_2_) | copy-start | bytes 2359300
  293.9 33.7 %collective-permute-start.24 = (bf16[4,192,512]{2,1,0:T(8,128)(2,1)S(1)}, bf16[4,192,512]{2,1,0:T(8,128)(2,1)S(1)}, u32[]{:S(2)}, u32[]{:S(2)}) collective-permute-start(bf16[4,192,512]{2,1,0:T(8,128)(2,1)S(1)} %collective-permute-done.23.refs_2_), channel_id=1, source_target_pairs={{0,16},{16,24},{24,8},{8,0},{1,17},{17,25},{25,9},{9,1},{2,18},{18... | collective-permute-start | bytes 2359304 | tf_op jit(solution)/shard_map/ppermute | solution.py:57
  310.8 24.2 %copy-start.17 = (bf16[4,192,512]{2,1,0:T(8,128)(2,1)}, bf16[4,192,512]{2,1,0:T(8,128)(2,1)S(1)}, u32[]{:S(2)}) copy-start(bf16[4,192,512]{2,1,0:T(8,128)(2,1)S(1)} %collective-permute-done.27.refs_2_) | copy-start | bytes 2359300
  310.8 31.6 %collective-permute-start.28 = (bf16[4,192,512]{2,1,0:T(8,128)(2,1)S(1)}, bf16[4,192,512]{2,1,0:T(8,128)(2,1)S(1)}, u32[]{:S(2)}, u32[]{:S(2)}) collective-permute-start(bf16[4,192,512]{2,1,0:T(8,128)(2,1)S(1)} %collective-permute-done.27.refs_2_), channel_id=1, source_target_pairs={{0,16},{16,24},{24,8},{8,0},{1,17},{17,25},{25,9},{9,1},{2,18},{18... | collective-permute-start | bytes 2359304 | tf_op jit(solution)/shard_map/ppermute | solution.py:57
  335.0 27.8 %collective-permute-start.29 = (bf16[272,2048]{1,0:T(8,128)(2,1)}, bf16[272,2048]{1,0:T(8,128)(2,1)S(1)}, u32[]{:S(2)}, u32[]{:S(2)}) collective-permute-start(bf16[272,2048]{1,0:T(8,128)(2,1)} %bitcast.17), channel_id=1, source_target_pairs={{0,4},{4,0},{1,5},{5,1},{2,6},{6,2},{3,7},{7,3},{8,12},{12,8},{9,1... | collective-permute-start | bytes 3342344 | tf_op jit(solution)/shard_map/ppermute | solution.py:506
  349.7 31.8 %collective-permute-start.30 = (bf16[272,2048]{1,0:T(8,128)(2,1)}, bf16[272,2048]{1,0:T(8,128)(2,1)S(1)}, u32[]{:S(2)}, u32[]{:S(2)}) collective-permute-start(bf16[272,2048]{1,0:T(8,128)(2,1)} %bitcast.18), channel_id=1, source_target_pairs={{0,4},{4,0},{1,5},{5,1},{2,6},{6,2},{3,7},{7,3},{8,12},{12,8},{9,1... | collective-permute-start | bytes 3342344 | tf_op jit(solution)/shard_map/ppermute | solution.py:506
  353.0 34.8 %collective-permute-start.31 = (bf16[3,64,512]{2,1,0:T(8,128)(2,1)}, bf16[3,64,512]{2,1,0:T(8,128)(2,1)S(1)}, u32[]{:S(2)}, u32[]{:S(2)}) collective-permute-start(bf16[3,64,512]{2,1,0:T(8,128)(2,1)} %get-tuple-element.64), channel_id=1, source_target_pairs={{0,1},{1,0},{2,3},{3,2},{4,5},{5,4},{6,7},{7,6},{8,9},{9,8},{10,11... | collective-permute-start | bytes 589832 | tf_op jit(solution)/shard_map/ppermute | solution.py:354
  353.0 34.8 %collective-permute-start.32 = (bf16[3,64,512]{2,1,0:T(8,128)(2,1)}, bf16[3,64,512]{2,1,0:T(8,128)(2,1)S(1)}, u32[]{:S(2)}, u32[]{:S(2)}) collective-permute-start(bf16[3,64,512]{2,1,0:T(8,128)(2,1)} %get-tuple-element.65), channel_id=1, source_target_pairs={{0,2},{1,3},{2,0},{3,1},{4,6},{5,7},{6,4},{7,5},{8,10},{9,11},{10,... | collective-permute-start | bytes 589832 | tf_op jit(solution)/shard_map/ppermute | solution.py:354
  353.6 34.2 %collective-permute-start.33 = (bf16[3,64,512]{2,1,0:T(8,128)(2,1)}, bf16[3,64,512]{2,1,0:T(8,128)(2,1)S(1)}, u32[]{:S(2)}, u32[]{:S(2)}) collective-permute-start(bf16[3,64,512]{2,1,0:T(8,128)(2,1)} %get-tuple-element.66), channel_id=1, source_target_pairs={{0,3},{1,2},{2,1},{3,0},{4,7},{5,6},{6,5},{7,4},{8,11},{9,10},{10,... | collective-permute-start | bytes 589832 | tf_op jit(solution)/shard_map/ppermute | solution.py:354
  362.8 18.7 %copy-start.4 = (bf16[272,2048]{1,0:T(8,128)(2,1)}, bf16[272,2048]{1,0:T(8,128)(2,1)S(1)}, u32[]{:S(2)}) copy-start(bf16[272,2048]{1,0:T(8,128)(2,1)S(1)} %collective-permute-done.29.refs_2_) | copy-start | bytes 3342340
  (18 other events, 68.2 us)
Sparse Core Ops, SparseCore 0:
  115.3 162.0 reduce-scatter.1
